TPU v7x, 256 devices: a whole 4x4x8 slice. The times are simulated.
256 devices in a mesh: section: 2 (over core), expert: 128 (over z, y, x).
Axes of the slice: x: 4, y: 4, z: 8, core: 2. Of those that a mesh axis runs over, the one named last changes fastest.
Arguments:
- tokens_in: bfloat16 [2, 8192, 3584], P(None, 'expert'), may hold values from -6 to 6
- route_ids: int32 [2, 2, 8192, 1], P('section', None, 'expert'), may hold values from 0 to 63; in each aligned block of 64 rows (0 to 63, 64 to 127, ..., all dimensions but the last counted through in order) at most 2 rows name the same one
- norm_gain: bfloat16 [2, 3584], P('section', 'expert'), may hold values from 0.099609375 to 1.8984375
- router: bfloat16 [2, 3584, 64], P('section', 'expert'), may hold values from -0.1875 to 0.1875
- gate_proj: bfloat16 [2, 3584, 65536], P('section', None, 'expert'), may hold values from -0.09375 to 0.09375
- up_proj: bfloat16 [2, 3584, 65536], P('section', None, 'expert'), may hold values from -0.09375 to 0.09375
- down_proj: bfloat16 [2, 65536, 3584], P('section', 'expert'), may hold values from -0.1875 to 0.1875
Outputs:
- layer_out: bfloat16 [2, 2, 8192, 3584], P('section', None, 'expert')
Inputs may be any that keep to these rules, and one draw needn't show every extreme that they name: `route_ids`: in each layer and micro-batch, the 64 tokens of one device (aligned blocks of 64 rows) name no expert more than 2 times, and in some of these blocks one expert exactly 2 times; the 1 ids of a token differ.
All inputs are finite; a program needn't handle non-finite values.
Results may differ from a plain program's by a relative error of at most 0.006.
Values may be sent and summed in bfloat16 or wider, within the bound.
A program may use at most 128 MiB of HBM per device.

v0:
```python
import jax
import jax.numpy as jnp
from jax import lax
from jax.sharding import PartitionSpec as P

HE = 1024


def shifted(block, axis, distance):
    devices = range(lax.axis_size(axis))
    route = [(i - distance, i) for i in devices if i - distance in devices]
    return lax.ppermute(block, axis, route)


def expert_rows(rows_in, gate_part, up_part, down_part):
    pre_gate = jnp.dot(rows_in, gate_part, preferred_element_type=jnp.float32)
    pre_up = jnp.dot(rows_in, up_part, preferred_element_type=jnp.float32)
    activated = (jax.nn.silu(pre_gate) * pre_up).astype(jnp.bfloat16)
    return jnp.dot(activated, down_part, preferred_element_type=jnp.float32).astype(jnp.bfloat16)


def on_device(tokens_in, route_ids, norm_gain, router, gate_proj, up_proj, down_proj):
    devices = lax.axis_size("expert")
    micro_count = tokens_in.shape[0]
    tok_rows = tokens_in.shape[1]
    model_width = tokens_in.shape[2]
    slice_units = gate_proj.shape[2]
    split_count = HE // slice_units
    expert_count = devices // split_count
    top_slots = route_ids.shape[3]
    capacity = 2 * tok_rows * top_slots // expert_count
    pair_count = tok_rows * top_slots
    section_index = lax.axis_index("section")
    gain_full, router_full = (
        lax.all_gather(norm_gain[0], "expert", axis=0, tiled=True),
        lax.all_gather(router[0], "expert", axis=0, tiled=True),
    )
    gain_wide = gain_full.astype(jnp.float32)
    gate_part = gate_proj[0]
    up_part = up_proj[0]
    down_part = down_proj[0]
    slot_ids = jnp.arange(expert_count * capacity, dtype=jnp.int32)
    expert_ids = jnp.arange(expert_count, dtype=jnp.int32)

    def moe_layer(hidden_in, ids_now):
        widened = hidden_in.astype(jnp.float32)
        inv_rms = lax.rsqrt(jnp.mean(widened * widened, axis=-1, keepdims=True) + 1e-06)
        normed = (widened * inv_rms * gain_wide).astype(jnp.bfloat16)
        logits = jnp.dot(normed, router_full, preferred_element_type=jnp.float32)
        chosen = ids_now[:, :, None] == expert_ids[None, None, :]
        weights = jax.nn.sigmoid(jnp.sum(jnp.where(chosen, logits[:, None, :], 0.0), axis=-1))
        flat_hit = chosen.reshape(pair_count, expert_count).astype(jnp.int32)
        before = jnp.cumsum(flat_hit, axis=0) - flat_hit
        rank_in = jnp.sum(before * flat_hit, axis=-1)
        target = ids_now.reshape(pair_count) * capacity + rank_in
        placed = (
            (slot_ids[:, None] == target[None, :])
            .astype(jnp.bfloat16)
            .reshape(expert_count, capacity, pair_count)
        )
        pair_rows = normed[:, None, :].reshape(pair_count, model_width)
        outgoing = jnp.einsum(
            "ecp,pd->ecd", placed, pair_rows, preferred_element_type=jnp.float32
        ).astype(jnp.bfloat16)
        copies = jnp.broadcast_to(
            outgoing[:, None], (expert_count, split_count, capacity, model_width)
        ).reshape(devices * capacity, model_width)
        arrived = lax.all_to_all(copies, "expert", split_axis=0, concat_axis=0, tiled=True)
        partial_value = expert_rows(arrived, gate_part, up_part, down_part)
        returned = lax.all_to_all(partial_value, "expert", split_axis=0, concat_axis=0, tiled=True)
        summed = jnp.sum(
            returned.reshape(expert_count, split_count, capacity, model_width).astype(jnp.float32),
            axis=1,
        ).astype(jnp.bfloat16)
        expert_out = jnp.einsum("ecp,ecd->pd", placed, summed, preferred_element_type=jnp.float32)
        spread_out = expert_out.reshape(tok_rows, top_slots, model_width)
        mixed_rows = widened + jnp.sum(weights[:, :, None] * spread_out, axis=1)
        return mixed_rows.astype(jnp.bfloat16)

    ids_all = route_ids[0]
    first_pass = jnp.stack(
        [
            moe_layer(tokens_in[micro_index], ids_all[micro_index])
            for micro_index in range(micro_count)
        ]
    )
    moved_batch = shifted(first_pass, "section", 1)
    second = jnp.stack(
        [
            moe_layer(moved_batch[micro_index], ids_all[micro_index])
            for micro_index in range(micro_count)
        ]
    )
    result = jnp.where(section_index == 0, first_pass, second)
    return result[None]


def solution(mesh):
    return jax.shard_map(
        on_device,
        mesh=mesh,
        in_specs=(
            P(None, "expert", None),
            P("section", None, "expert", None),
            P("section", "expert"),
            P("section", "expert", None),
            P("section", None, "expert"),
            P("section", None, "expert"),
            P("section", "expert", None),
        ),
        out_specs=P("section", None, "expert", None),
        check_vma=False,
    )
```

profile of v0, /device:TPU:1, one launch (start us, length us, event | category | flops | bytes accessed | tf_op | source)
XLA Modules:
  0.0 1135.0 jit_solution(4421476428468735068)
XLA Ops:
  4.1 302.7 %all-reduce = bf16[3584]{0:T(1024)(128)(2,1)S(1)} all-reduce(bf16[3584]{0:T(1024)(128)(2,1)S(1)} %dynamic-update-slice), channel_id=2, replica_groups=mesh['section'=2,'expert'=128] {'expert'}, use_global_device_ids=true, to_apply=%add | all-reduce | flops 3584 | bytes 14336
  312.7 6.2 all-to-all-start
  320.4 26.5 %all-to-all-done = bf16[128,2,3584]{2,1,0:T(2,128)(2,1)S(1)} async-done(((bf16[128,2,3584]{2,1,0:T(2,128)(2,1)}), bf16[128,2,3584]{2,1,0:T(2,128)(2,1)S(1)}, u32[]{:S(2)}, u32[]{:S(2)}) %all-to-all-start) | async-done | bytes 1835040 | tf_op jit(solution)/shard_map/all_to_all | solution.py:68
  349.1 6.8 all-to-all-start.2
  355.9 4.9 all_to_all.58
  364.5 7.1 convolution_convert_fusion.3
  371.7 4.7 all_to_all.59
  376.4 7.5 all-to-all-done.2
  383.9 7.5 all-to-all-start.1
  393.1 3.8 fusion.34
  396.9 6.6 convolution_convert_fusion.2
  403.5 4.8 all_to_all.64
  408.3 16.2 %all-to-all-done.1 = bf16[128,2,3584]{2,1,0:T(2,128)(2,1)} async-done(((bf16[128,2,3584]{2,1,0:T(2,128)(2,1)}), bf16[128,2,3584]{2,1,0:T(2,128)(2,1)}, u32[]{:S(2)}, u32[]{:S(2)}) %all-to-all-start.1) | async-done | bytes 1835040 | tf_op jit(solution)/shard_map/all_to_all | solution.py:70
  424.5 6.5 all-to-all-start.3
  431.0 348.1 %all-gather.1 = bf16[1,3584,64]{2,0,1:T(2,128)(2,1)} all-gather(bf16[1,28,64]{2,0,1:T(2,128)(2,1)S(1)} %copy.37), channel_id=3, replica_groups=mesh['section'=2,'expert'=128] {'expert'}, dimensions={1}, use_global_device_ids=true | all-gather | bytes 462336 | tf_op jit(solution)/shard_map/all_gather | solution.py:36
  783.6 4.5 bitcast_reduce_fusion.3
  792.7 115.6 %collective-permute-done = bf16[2,64,3584]{2,1,0:T(8,128)(2,1)S(1)} collective-permute-done((bf16[2,64,3584]{2,1,0:T(8,128)(2,1)S(1)}, bf16[2,64,3584]{2,1,0:T(8,128)(2,1)S(1)}, u32[]{:S(2)}, u32[]{:S(2)}) %collective-permute-start) | collective-permute-done | bytes 917536 | tf_op jit(solution)/shard_map/ppermute | solution.py:12
  912.3 9.9 all-to-all-start.4
  923.7 43.6 %all-to-all-done.4 = bf16[128,2,3584]{2,1,0:T(2,128)(2,1)S(1)} async-done(((bf16[128,2,3584]{2,1,0:T(2,128)(2,1)}), bf16[128,2,3584]{2,1,0:T(2,128)(2,1)S(1)}, u32[]{:S(2)}, u32[]{:S(2)}) %all-to-all-start.4) | async-done | bytes 1835040 | tf_op jit(solution)/shard_map/all_to_all | solution.py:68
  969.5 9.1 all-to-all-start.6
  980.3 3.8 fusion.32
  984.2 6.6 convolution_convert_fusion.1
  990.8 4.8 all_to_all.69
  995.6 26.3 %all-to-all-done.6 = bf16[128,2,3584]{2,1,0:T(2,128)(2,1)} async-done(((bf16[128,2,3584]{2,1,0:T(2,128)(2,1)}), bf16[128,2,3584]{2,1,0:T(2,128)(2,1)}, u32[]{:S(2)}, u32[]{:S(2)}) %all-to-all-start.6) | async-done | bytes 1835040 | tf_op jit(solution)/shard_map/all_to_all | solution.py:68
  1021.9 9.8 all-to-all-start.5
  1031.7 4.9 all_to_all.73
  1040.3 7.1 convolution_convert_fusion
  1047.5 4.7 all_to_all.74
  1052.2 22.5 %all-to-all-done.5 = bf16[128,2,3584]{2,1,0:T(2,128)(2,1)S(1)} async-done(((bf16[128,2,3584]{2,1,0:T(2,128)(2,1)}), bf16[128,2,3584]{2,1,0:T(2,128)(2,1)S(1)}, u32[]{:S(2)}, u32[]{:S(2)}) %all-to-all-start.5) | async-done | bytes 1835040 | tf_op jit(solution)/shard_map/all_to_all | solution.py:70
  1074.7 10.6 all-to-all-start.7
  1091.4 36.7 %all-to-all-done.7 = bf16[128,2,3584]{2,1,0:T(2,128)(2,1)} async-done(((bf16[128,2,3584]{2,1,0:T(2,128)(2,1)}), bf16[128,2,3584]{2,1,0:T(2,128)(2,1)}, u32[]{:S(2)}, u32[]{:S(2)}) %all-to-all-start.7) | async-done | bytes 1835040 | tf_op jit(solution)/shard_map/all_to_all | solution.py:70
  1128.1 4.5 bitcast_reduce_fusion
  (81 shorter events, 48.4 us)
Async XLA Ops:
  0.0 309.0 %copy-start.1 = (bf16[2,64,3584]{2,1,0:T(8,128)(2,1)S(1)}, bf16[2,64,3584]{2,1,0:T(8,128)(2,1)}, u32[]{:S(2)}) copy-start(bf16[2,64,3584]{2,1,0:T(8,128)(2,1)} %param.7) | copy-start | bytes 2752516
  312.7 34.1 %all-to-all-start = ((bf16[128,2,3584]{2,1,0:T(2,128)(2,1)}), bf16[128,2,3584]{2,1,0:T(2,128)(2,1)S(1)}, u32[]{:S(2)}, u32[]{:S(2)}) async-start(bf16[128,2,3584]{2,1,0:T(2,128)(2,1)} %bitcast.239), calls=%async_computation | async-start | bytes 3670016 | tf_op jit(solution)/shard_map/all_to_all | solution.py:68
  346.9 2.2 copy-start
  349.1 34.8 %all-to-all-start.2 = ((bf16[128,2,3584]{2,1,0:T(2,128)(2,1)}), bf16[128,2,3584]{2,1,0:T(2,128)(2,1)S(1)}, u32[]{:S(2)}, u32[]{:S(2)}) async-start(bf16[128,2,3584]{2,1,0:T(2,128)(2,1)} %bitcast.236), calls=%async_computation.2 | async-start | bytes 3670016 | tf_op jit(solution)/shard_map/all_to_all | solution.py:68
  383.9 40.6 %all-to-all-start.1 = ((bf16[128,2,3584]{2,1,0:T(2,128)(2,1)}), bf16[128,2,3584]{2,1,0:T(2,128)(2,1)}, u32[]{:S(2)}, u32[]{:S(2)}) async-start(bf16[128,2,3584]{2,1,0:T(2,128)(2,1)} %all_to_all.59), calls=%async_computation.1 | async-start | bytes 3670016 | tf_op jit(solution)/shard_map/all_to_all | solution.py:70
  393.1 3.8 copy-start.5
  408.3 22.7 %copy-start.11 = (bf16[1,28,64]{2,1,0:T(8,128)(2,1)S(1)}, bf16[1,28,64]{2,1,0:T(8,128)(2,1)}, u32[]{:S(2)}) copy-start(bf16[1,28,64]{2,1,0:T(8,128)(2,1)} %param.10) | copy-start | bytes 10756
  424.5 364.0 %all-to-all-start.3 = ((bf16[128,2,3584]{2,1,0:T(2,128)(2,1)}), bf16[128,2,3584]{2,1,0:T(2,128)(2,1)S(1)}, u32[]{:S(2)}, u32[]{:S(2)}) async-start(bf16[128,2,3584]{2,1,0:T(2,128)(2,1)} %all_to_all.64), calls=%async_computation.3 | async-start | bytes 3670016 | tf_op jit(solution)/shard_map/all_to_all | solution.py:70
  431.0 351.8 %copy-start.2 = (bf16[2,64,3584]{2,1,0:T(8,128)(2,1)S(1)}, bf16[2,64,3584]{2,1,0:T(8,128)(2,1)}, u32[]{:S(2)}) copy-start(bf16[2,64,3584]{2,1,0:T(8,128)(2,1)} %param.7) | copy-start | bytes 2752516
  782.8 0.8 copy-start.10
  791.3 117.3 %copy-start.7 = (bf16[1,64,3584]{2,1,0:T(8,128)(2,1)}, bf16[1,64,3584]{2,1,0:T(8,128)(2,1)S(1)}, u32[]{:S(2)}) copy-start(bf16[1,64,3584]{2,1,0:T(8,128)(2,1)S(1)} %fusion.13) | copy-start | bytes 1376260
  791.4 116.9 %collective-permute-start = (bf16[2,64,3584]{2,1,0:T(8,128)(2,1)S(1)}, bf16[2,64,3584]{2,1,0:T(8,128)(2,1)S(1)}, u32[]{:S(2)}, u32[]{:S(2)}) collective-permute-start(bf16[2,64,3584]{2,1,0:T(8,128)(2,1)S(1)} %pad_maximum_fusion), channel_id=1, source_target_pairs={{0,128},{1,129},{2,130},{3,131},{4,132},{5,133},{6,134},{7,135},{8... | collective-permute-start | bytes 2752520 | tf_op jit(solution)/shard_map/ppermute | solution.py:12
  908.3 13.9 %copy-start.3 = (bf16[2,64,3584]{2,1,0:T(8,128)(2,1)}, bf16[2,64,3584]{2,1,0:T(8,128)(2,1)S(1)}, u32[]{:S(2)}) copy-start(bf16[2,64,3584]{2,1,0:T(8,128)(2,1)S(1)} %collective-permute-done) | copy-start | bytes 2752516
  912.3 55.0 %all-to-all-start.4 = ((bf16[128,2,3584]{2,1,0:T(2,128)(2,1)}), bf16[128,2,3584]{2,1,0:T(2,128)(2,1)S(1)}, u32[]{:S(2)}, u32[]{:S(2)}) async-start(bf16[128,2,3584]{2,1,0:T(2,128)(2,1)} %bitcast.238), calls=%async_computation.4 | async-start | bytes 3670016 | tf_op jit(solution)/shard_map/all_to_all | solution.py:68
  969.5 52.4 %all-to-all-start.6 = ((bf16[128,2,3584]{2,1,0:T(2,128)(2,1)}), bf16[128,2,3584]{2,1,0:T(2,128)(2,1)}, u32[]{:S(2)}, u32[]{:S(2)}) async-start(bf16[128,2,3584]{2,1,0:T(2,128)(2,1)} %bitcast.237), calls=%async_computation.6 | async-start | bytes 3670016 | tf_op jit(solution)/shard_map/all_to_all | solution.py:68
  980.3 3.8 copy-start.6
  1021.9 52.9 %all-to-all-start.5 = ((bf16[128,2,3584]{2,1,0:T(2,128)(2,1)}), bf16[128,2,3584]{2,1,0:T(2,128)(2,1)S(1)}, u32[]{:S(2)}, u32[]{:S(2)}) async-start(bf16[128,2,3584]{2,1,0:T(2,128)(2,1)} %all_to_all.69), calls=%async_computation.5 | async-start | bytes 3670016 | tf_op jit(solution)/shard_map/all_to_all | solution.py:70
  1052.2 33.2 %copy-start.4 = (bf16[2,64,3584]{2,1,0:T(8,128)(2,1)S(1)}, bf16[2,64,3584]{2,1,0:T(8,128)(2,1)}, u32[]{:S(2)}) copy-start(bf16[2,64,3584]{2,1,0:T(8,128)(2,1)} %copy-done.3) | copy-start | bytes 2752516
  1074.7 53.4 %all-to-all-start.7 = ((bf16[128,2,3584]{2,1,0:T(2,128)(2,1)}), bf16[128,2,3584]{2,1,0:T(2,128)(2,1)}, u32[]{:S(2)}, u32[]{:S(2)}) async-start(bf16[128,2,3584]{2,1,0:T(2,128)(2,1)} %all_to_all.74), calls=%async_computation.7 | async-start | bytes 3670016 | tf_op jit(solution)/shard_map/all_to_all | solution.py:70
  1091.4 41.2 %copy-start.9 = (bf16[64,2,3584]{2,1,0:T(2,128)(2,1)S(1)}, bf16[64,2,3584]{2,1,0:T(2,128)(2,1)}, u32[]{:S(2)}) copy-start(bf16[64,2,3584]{2,1,0:T(2,128)(2,1)} %bitcast_reduce_fusion.1) | copy-start | bytes 2752516
  1132.7 1.0 copy-start.8
where the time goes:
time: 1150 us; the launch traced here: 1130 us
  blocking collectives  651 us (57%)
  waiting for transfers between devices  295 us (26%)
  starting transfers between devices  67.8 us (6%)
  local copies, waits for them, and re-layouts  51.9 us (5%)
  matrix products  49.7 us (4%)
  other arithmetic  18.5 us (2%)
    all_gather x1, blocking collectives, on_device(): lax.all_gather(router[0], 'expert', axis=0, tiled=True)  348 us
    unnamed x1, blocking collectives  303 us
    ppermute x1, waiting for transfers between devices, shifted(): return lax.ppermute(block, axis, route)  116 us
    all_to_all x4, waiting for transfers between devices, moe_layer(): lax.all_to_all(copies, 'expert', split_axis=0, concat_axis=0, tiled=True)  104 us
    all_to_all x4, waiting for transfers between devices, moe_layer(): lax.all_to_all(partial_value, 'expert', split_axis=0, concat_axis=0, tile...  75.4 us
    all_to_all x4, starting transfers between devices, moe_layer(): lax.all_to_all(partial_value, 'expert', split_axis=0, concat_axis=0, tile...  34.5 us
    all_to_all x4, starting transfers between devices, moe_layer(): lax.all_to_all(copies, 'expert', split_axis=0, concat_axis=0, tiled=True)  32 us
    dot_general x4, matrix products, expert_rows(): jnp.dot(activated, down_part, preferred_element_type=jnp.float32)  27.5 us
  transfers between devices with their start and end apart: 9, of which 8 were waited for; matrix products, arithmetic and copies ran while one was open for 5% of the time, Pallas kernels for 0%

commit v1 on v0

--- a/solution.py
+++ b/solution.py
@@ -31,10 +31,11 @@
     capacity = 2 * tok_rows * top_slots // expert_count
     pair_count = tok_rows * top_slots
     section_index = lax.axis_index("section")
-    gain_full, router_full = (
-        lax.all_gather(norm_gain[0], "expert", axis=0, tiled=True),
-        lax.all_gather(router[0], "expert", axis=0, tiled=True),
-    )
+    share = jnp.concatenate([router[0], norm_gain[0][:, None]], axis=1)
+    spread = jnp.broadcast_to(share[None], (devices,) + share.shape)
+    gathered = lax.all_to_all(spread, "expert", split_axis=0, concat_axis=0, tiled=True)
+    gathered = gathered.reshape(model_width, share.shape[1])
+    gain_full, router_full = gathered[:, -1], gathered[:, :-1]
     gain_wide = gain_full.astype(jnp.float32)
     gate_part = gate_proj[0]
     up_part = up_proj[0]

time: 1150 us -> 515 us (0.45)
  the two profiles are of different devices: /device:TPU:1 before, /device:TPU:32 now
where the time goes in v1:
time: 515 us; the launch traced here: 506 us
  waiting for transfers between devices  295 us (57%)
  starting transfers between devices  79.1 us (15%)
  matrix products  57 us (11%)
  local copies, waits for them, and re-layouts  56.4 us (11%)
  other arithmetic  17.2 us (3%)
    all_to_all x4, waiting for transfers between devices, moe_layer(): lax.all_to_all(copies, 'expert', split_axis=0, concat_axis=0, tiled=True)  141 us
    all_to_all x4, waiting for transfers between devices, moe_layer(): lax.all_to_all(partial_value, 'expert', split_axis=0, concat_axis=0, tile...  133 us
    all_to_all x4, starting transfers between devices, moe_layer(): lax.all_to_all(partial_value, 'expert', split_axis=0, concat_axis=0, tile...  35.5 us
    dot_general x4, matrix products, expert_rows(): jnp.dot(activated, down_part, preferred_element_type=jnp.float32)  28 us
    all_to_all x4, starting transfers between devices, moe_layer(): lax.all_to_all(copies, 'expert', split_axis=0, concat_axis=0, tiled=True)  27.2 us
    all_to_all x1, waiting for transfers between devices, on_device(): lax.all_to_all(spread, 'expert', split_axis=0, concat_axis=0, tiled=True)  19.4 us
    all_to_all x4, local copies, waits for them, and re-layouts, moe_layer(): lax.all_to_all(partial_value, 'expert', split_axis=0, concat_axis=0, tile...  19.1 us
    dot_general x4, matrix products, expert_rows(): pre_gate = jnp.dot(rows_in, gate_part, preferred_element_type=jnp.float32)  18.3 us
  transfers between devices with their start and end apart: 10, of which 10 were waited for; matrix products, arithmetic and copies ran while one was open for 13% of the time, Pallas kernels for 0%

profile of v1, /device:TPU:32, one launch (start us, length us, event | category | flops | bytes accessed | tf_op | source)
XLA Modules:
  0.0 506.0 jit_solution(17548055759525029983)
XLA Ops:
  4.0 15.0 %all-to-all-start = ((bf16[128,2,910]{2,1,0:T(2,128)(2,1)}), bf16[128,2,910]{2,1,0:T(2,128)(2,1)S(1)}, u32[]{:S(2)}, u32[]{:S(2)}) async-start(bf16[128,2,910]{2,1,0:T(2,128)(2,1)} %reshape.399), calls=%async_computation | async-start | bytes 1048576 | tf_op jit(solution)/shard_map/all_to_all | solution.py:36
  20.0 19.4 %all-to-all-done = bf16[128,2,910]{2,1,0:T(2,128)(2,1)S(1)} async-done(((bf16[128,2,910]{2,1,0:T(2,128)(2,1)}), bf16[128,2,910]{2,1,0:T(2,128)(2,1)S(1)}, u32[]{:S(2)}, u32[]{:S(2)}) %all-to-all-start) | async-done | bytes 465952 | tf_op jit(solution)/shard_map/all_to_all | solution.py:36
  47.0 6.9 %all-to-all-start.3 = ((bf16[128,2,3584]{2,1,0:T(2,128)(2,1)}), bf16[128,2,3584]{2,1,0:T(2,128)(2,1)S(1)}, u32[]{:S(2)}, u32[]{:S(2)}) async-start(bf16[128,2,3584]{2,1,0:T(2,128)(2,1)} %bitcast.230), calls=%async_computation.3 | async-start | bytes 3670016 | tf_op jit(solution)/shard_map/all_to_all | solution.py:69
  57.3 42.8 %all-to-all-done.3 = bf16[128,2,3584]{2,1,0:T(2,128)(2,1)S(1)} async-done(((bf16[128,2,3584]{2,1,0:T(2,128)(2,1)}), bf16[128,2,3584]{2,1,0:T(2,128)(2,1)S(1)}, u32[]{:S(2)}, u32[]{:S(2)}) %all-to-all-start.3) | async-done | bytes 1835040 | tf_op jit(solution)/shard_map/all_to_all | solution.py:69
  104.2 6.4 %all-to-all-start.1 = ((bf16[128,2,3584]{2,1,0:T(2,128)(2,1)}), bf16[128,2,3584]{2,1,0:T(2,128)(2,1)S(1)}, u32[]{:S(2)}, u32[]{:S(2)}) async-start(bf16[128,2,3584]{2,1,0:T(2,128)(2,1)} %bitcast.227), calls=%async_computation.1 | async-start | bytes 3670016 | tf_op jit(solution)/shard_map/all_to_all | solution.py:69
  110.6 4.9 all_to_all.67
  120.0 7.3 %convolution_convert_fusion.2 = bf16[256,3584]{1,0:T(8,128)(2,1)} fusion(bf16[1,512,3584]{2,1,0:T(8,128)(2,1)} %param.13, bf16[256,3584]{1,0:T(8,128)(2,1)} %all_to_all.67, bf16[1,3584,512]{2,1,0:T(8,128)(2,1)} %param.12, f32[256,512]{1,0:T(8,128)} %fusion.34), kind=kOutput, calls=%fused_computation.2 | convolution fusion | flops 1880752128 | bytes 11534336 | tf_op jit(solution)/shard_map/dot_general | solution.py:19
  127.3 4.8 all_to_all.68
  132.1 24.6 %all-to-all-done.1 = bf16[128,2,3584]{2,1,0:T(2,128)(2,1)S(1)} async-done(((bf16[128,2,3584]{2,1,0:T(2,128)(2,1)}), bf16[128,2,3584]{2,1,0:T(2,128)(2,1)S(1)}, u32[]{:S(2)}, u32[]{:S(2)}) %all-to-all-start.1) | async-done | bytes 1835040 | tf_op jit(solution)/shard_map/all_to_all | solution.py:69
  156.7 6.8 %all-to-all-start.4 = ((bf16[128,2,3584]{2,1,0:T(2,128)(2,1)}), bf16[128,2,3584]{2,1,0:T(2,128)(2,1)}, u32[]{:S(2)}, u32[]{:S(2)}) async-start(bf16[128,2,3584]{2,1,0:T(2,128)(2,1)} %all_to_all.68), calls=%async_computation.4 | async-start | bytes 3670016 | tf_op jit(solution)/shard_map/all_to_all | solution.py:71
  165.2 4.6 fusion.36
  169.8 6.8 %convolution_convert_fusion.3 = bf16[256,3584]{1,0:T(8,128)(2,1)} fusion(bf16[1,512,3584]{2,1,0:T(8,128)(2,1)} %param.13, bf16[256,3584]{1,0:T(8,128)(2,1)S(1)} %copy-done.7, bf16[1,3584,512]{2,1,0:T(8,128)(2,1)} %param.12, f32[256,512]{1,0:T(8,128)} %fusion.36), kind=kOutput, calls=%fused_computation.3 | convolution fusion | flops 1880752128 | bytes 11534336 | tf_op jit(solution)/shard_map/dot_general | solution.py:19
  176.6 4.8 all_to_all.63
  181.3 27.7 %all-to-all-done.4 = bf16[128,2,3584]{2,1,0:T(2,128)(2,1)} async-done(((bf16[128,2,3584]{2,1,0:T(2,128)(2,1)}), bf16[128,2,3584]{2,1,0:T(2,128)(2,1)}, u32[]{:S(2)}, u32[]{:S(2)}) %all-to-all-start.4) | async-done | bytes 1835040 | tf_op jit(solution)/shard_map/all_to_all | solution.py:71
  209.0 14.9 %all-to-all-start.2 = ((bf16[128,2,3584]{2,1,0:T(2,128)(2,1)}), bf16[128,2,3584]{2,1,0:T(2,128)(2,1)S(1)}, u32[]{:S(2)}, u32[]{:S(2)}) async-start(bf16[128,2,3584]{2,1,0:T(2,128)(2,1)} %all_to_all.63), calls=%async_computation.2 | async-start | bytes 3670016 | tf_op jit(solution)/shard_map/all_to_all | solution.py:71
  225.9 4.5 bitcast_reduce_fusion.2
  230.9 37.9 %all-to-all-done.2 = bf16[128,2,3584]{2,1,0:T(2,128)(2,1)S(1)} async-done(((bf16[128,2,3584]{2,1,0:T(2,128)(2,1)}), bf16[128,2,3584]{2,1,0:T(2,128)(2,1)S(1)}, u32[]{:S(2)}, u32[]{:S(2)}) %all-to-all-start.2) | async-done | bytes 1835040 | tf_op jit(solution)/shard_map/all_to_all | solution.py:71
  279.6 6.9 %all-to-all-start.5 = ((bf16[128,2,3584]{2,1,0:T(2,128)(2,1)}), bf16[128,2,3584]{2,1,0:T(2,128)(2,1)S(1)}, u32[]{:S(2)}, u32[]{:S(2)}) async-start(bf16[128,2,3584]{2,1,0:T(2,128)(2,1)} %bitcast.229), calls=%async_computation.5 | async-start | bytes 3670016 | tf_op jit(solution)/shard_map/all_to_all | solution.py:69
  289.9 44.7 %all-to-all-done.5 = bf16[128,2,3584]{2,1,0:T(2,128)(2,1)S(1)} async-done(((bf16[128,2,3584]{2,1,0:T(2,128)(2,1)}), bf16[128,2,3584]{2,1,0:T(2,128)(2,1)S(1)}, u32[]{:S(2)}, u32[]{:S(2)}) %all-to-all-start.5) | async-done | bytes 1835040 | tf_op jit(solution)/shard_map/all_to_all | solution.py:69
  338.0 7.0 %all-to-all-start.7 = ((bf16[128,2,3584]{2,1,0:T(2,128)(2,1)}), bf16[128,2,3584]{2,1,0:T(2,128)(2,1)}, u32[]{:S(2)}, u32[]{:S(2)}) async-start(bf16[128,2,3584]{2,1,0:T(2,128)(2,1)} %bitcast.228), calls=%async_computation.7 | async-start | bytes 3670016 | tf_op jit(solution)/shard_map/all_to_all | solution.py:69
  346.7 4.6 fusion.32
  351.3 6.7 %convolution_convert_fusion.1 = bf16[256,3584]{1,0:T(8,128)(2,1)} fusion(bf16[1,512,3584]{2,1,0:T(8,128)(2,1)} %param.13, bf16[256,3584]{1,0:T(8,128)(2,1)S(1)} %copy-done.8, bf16[1,3584,512]{2,1,0:T(8,128)(2,1)} %param.12, f32[256,512]{1,0:T(8,128)} %fusion.32), kind=kOutput, calls=%fused_computation.1 | convolution fusion | flops 1880752128 | bytes 11534336 | tf_op jit(solution)/shard_map/dot_general | solution.py:19
  358.0 4.7 all_to_all.73
  362.8 29.3 %all-to-all-done.7 = bf16[128,2,3584]{2,1,0:T(2,128)(2,1)} async-done(((bf16[128,2,3584]{2,1,0:T(2,128)(2,1)}), bf16[128,2,3584]{2,1,0:T(2,128)(2,1)}, u32[]{:S(2)}, u32[]{:S(2)}) %all-to-all-start.7) | async-done | bytes 1835040 | tf_op jit(solution)/shard_map/all_to_all | solution.py:69
  392.1 6.7 %all-to-all-start.6 = ((bf16[128,2,3584]{2,1,0:T(2,128)(2,1)}), bf16[128,2,3584]{2,1,0:T(2,128)(2,1)S(1)}, u32[]{:S(2)}, u32[]{:S(2)}) async-start(bf16[128,2,3584]{2,1,0:T(2,128)(2,1)} %all_to_all.73), calls=%async_computation.6 | async-start | bytes 3670016 | tf_op jit(solution)/shard_map/all_to_all | solution.py:71
  398.8 4.9 all_to_all.77
  408.2 7.2 %convolution_convert_fusion = bf16[256,3584]{1,0:T(8,128)(2,1)} fusion(bf16[1,512,3584]{2,1,0:T(8,128)(2,1)} %param.13, bf16[256,3584]{1,0:T(8,128)(2,1)} %all_to_all.77, bf16[1,3584,512]{2,1,0:T(8,128)(2,1)} %param.12, f32[256,512]{1,0:T(8,128)} %fusion.30), kind=kOutput, calls=%fused_computation | convolution fusion | flops 1880752128 | bytes 11534336 | tf_op jit(solution)/shard_map/dot_general | solution.py:19
  415.4 4.8 all_to_all.78
  420.2 25.4 %all-to-all-done.6 = bf16[128,2,3584]{2,1,0:T(2,128)(2,1)S(1)} async-done(((bf16[128,2,3584]{2,1,0:T(2,128)(2,1)}), bf16[128,2,3584]{2,1,0:T(2,128)(2,1)S(1)}, u32[]{:S(2)}, u32[]{:S(2)}) %all-to-all-start.6) | async-done | bytes 1835040 | tf_op jit(solution)/shard_map/all_to_all | solution.py:71
  445.6 7.2 %all-to-all-start.8 = ((bf16[128,2,3584]{2,1,0:T(2,128)(2,1)}), bf16[128,2,3584]{2,1,0:T(2,128)(2,1)}, u32[]{:S(2)}, u32[]{:S(2)}) async-start(bf16[128,2,3584]{2,1,0:T(2,128)(2,1)} %all_to_all.78), calls=%async_computation.8 | async-start | bytes 3670016 | tf_op jit(solution)/shard_map/all_to_all | solution.py:71
  457.2 41.7 %all-to-all-done.8 = bf16[128,2,3584]{2,1,0:T(2,128)(2,1)} async-done(((bf16[128,2,3584]{2,1,0:T(2,128)(2,1)}), bf16[128,2,3584]{2,1,0:T(2,128)(2,1)}, u32[]{:S(2)}, u32[]{:S(2)}) %all-to-all-start.8) | async-done | bytes 1835040 | tf_op jit(solution)/shard_map/all_to_all | solution.py:71
  498.8 4.5 bitcast_reduce_fusion
  (82 shorter events, 58.6 us)
Async XLA Ops:
  1.5 17.5 %copy-start.11 = (s32[1,2,64,1]{2,3,1,0:T(1,128)S(1)}, s32[1,2,64,1]{2,3,1,0:T(1,128)}, u32[]{:S(2)}) copy-start(s32[1,2,64,1]{2,3,1,0:T(1,128)} %param.8) | copy-start | bytes 1540
  1.7 18.0 %copy-start.1 = (bf16[2,64,3584]{2,1,0:T(8,128)(2,1)S(1)}, bf16[2,64,3584]{2,1,0:T(8,128)(2,1)}, u32[]{:S(2)}) copy-start(bf16[2,64,3584]{2,1,0:T(8,128)(2,1)} %param.7) | copy-start | bytes 2752516
  4.0 35.3 %all-to-all-start = ((bf16[128,2,910]{2,1,0:T(2,128)(2,1)}), bf16[128,2,910]{2,1,0:T(2,128)(2,1)S(1)}, u32[]{:S(2)}, u32[]{:S(2)}) async-start(bf16[128,2,910]{2,1,0:T(2,128)(2,1)} %reshape.399), calls=%async_computation | async-start | bytes 1048576 | tf_op jit(solution)/shard_map/all_to_all | solution.py:36
  47.0 53.1 %all-to-all-start.3 = ((bf16[128,2,3584]{2,1,0:T(2,128)(2,1)}), bf16[128,2,3584]{2,1,0:T(2,128)(2,1)S(1)}, u32[]{:S(2)}, u32[]{:S(2)}) async-start(bf16[128,2,3584]{2,1,0:T(2,128)(2,1)} %bitcast.230), calls=%async_computation.3 | async-start | bytes 3670016 | tf_op jit(solution)/shard_map/all_to_all | solution.py:69
  100.1 4.0 copy-start
  104.2 52.5 %all-to-all-start.1 = ((bf16[128,2,3584]{2,1,0:T(2,128)(2,1)}), bf16[128,2,3584]{2,1,0:T(2,128)(2,1)S(1)}, u32[]{:S(2)}, u32[]{:S(2)}) async-start(bf16[128,2,3584]{2,1,0:T(2,128)(2,1)} %bitcast.227), calls=%async_computation.1 | async-start | bytes 3670016 | tf_op jit(solution)/shard_map/all_to_all | solution.py:69
  156.7 52.3 %all-to-all-start.4 = ((bf16[128,2,3584]{2,1,0:T(2,128)(2,1)}), bf16[128,2,3584]{2,1,0:T(2,128)(2,1)}, u32[]{:S(2)}, u32[]{:S(2)}) async-start(bf16[128,2,3584]{2,1,0:T(2,128)(2,1)} %all_to_all.68), calls=%async_computation.4 | async-start | bytes 3670016 | tf_op jit(solution)/shard_map/all_to_all | solution.py:71
  165.2 4.6 copy-start.7
  209.0 59.8 %all-to-all-start.2 = ((bf16[128,2,3584]{2,1,0:T(2,128)(2,1)}), bf16[128,2,3584]{2,1,0:T(2,128)(2,1)S(1)}, u32[]{:S(2)}, u32[]{:S(2)}) async-start(bf16[128,2,3584]{2,1,0:T(2,128)(2,1)} %all_to_all.63), calls=%async_computation.2 | async-start | bytes 3670016 | tf_op jit(solution)/shard_map/all_to_all | solution.py:71
  223.9 1.6 copy-start.2
  268.8 2.3 copy-start.3
  271.5 4.9 copy-start.9
  271.6 3.4 collective-permute-start
  275.0 0.9 copy-start.4
  279.6 55.1 %all-to-all-start.5 = ((bf16[128,2,3584]{2,1,0:T(2,128)(2,1)}), bf16[128,2,3584]{2,1,0:T(2,128)(2,1)S(1)}, u32[]{:S(2)}, u32[]{:S(2)}) async-start(bf16[128,2,3584]{2,1,0:T(2,128)(2,1)} %bitcast.229), calls=%async_computation.5 | async-start | bytes 3670016 | tf_op jit(solution)/shard_map/all_to_all | solution.py:69
  338.0 54.0 %all-to-all-start.7 = ((bf16[128,2,3584]{2,1,0:T(2,128)(2,1)}), bf16[128,2,3584]{2,1,0:T(2,128)(2,1)}, u32[]{:S(2)}, u32[]{:S(2)}) async-start(bf16[128,2,3584]{2,1,0:T(2,128)(2,1)} %bitcast.228), calls=%async_computation.7 | async-start | bytes 3670016 | tf_op jit(solution)/shard_map/all_to_all | solution.py:69
  346.7 4.7 copy-start.8
  392.1 53.5 %all-to-all-start.6 = ((bf16[128,2,3584]{2,1,0:T(2,128)(2,1)}), bf16[128,2,3584]{2,1,0:T(2,128)(2,1)S(1)}, u32[]{:S(2)}, u32[]{:S(2)}) async-start(bf16[128,2,3584]{2,1,0:T(2,128)(2,1)} %all_to_all.73), calls=%async_computation.6 | async-start | bytes 3670016 | tf_op jit(solution)/shard_map/all_to_all | solution.py:71
  445.6 53.3 %all-to-all-start.8 = ((bf16[128,2,3584]{2,1,0:T(2,128)(2,1)}), bf16[128,2,3584]{2,1,0:T(2,128)(2,1)}, u32[]{:S(2)}, u32[]{:S(2)}) async-start(bf16[128,2,3584]{2,1,0:T(2,128)(2,1)} %all_to_all.78), calls=%async_computation.8 | async-start | bytes 3670016 | tf_op jit(solution)/shard_map/all_to_all | solution.py:71
  452.8 1.6 copy-start.5
  457.2 46.2 %copy-start.6 = (bf16[2,64,3584]{2,1,0:T(8,128)(2,1)S(1)}, bf16[2,64,3584]{2,1,0:T(8,128)(2,1)}, u32[]{:S(2)}) copy-start(bf16[2,64,3584]{2,1,0:T(8,128)(2,1)} %copy-done.4) | copy-start | bytes 2752516
  503.4 1.0 copy-start.10

commit v2 on v0

v2 whole, which is shorter than its diff:
```python
import functools

import jax
import jax.numpy as jnp
from jax import lax
from jax.experimental import pallas as pl
from jax.experimental.pallas import tpu as pltpu
from jax.sharding import PartitionSpec as P

MESH = pl.DeviceIdType.MESH
HE = 1024
MB = 2
RING_X, RING_Y, RING_Z = 4, 4, 8
PLANE = RING_Y * RING_Z
CHUNKS = 4
BF16 = jnp.bfloat16
F32 = jnp.float32


def landed(ref, sem):
    pltpu.make_async_copy(ref, ref, sem).wait()


def kernel(
    ids_ref, shared_ref, tokens_ref, gate_hbm, up_hbm, down_hbm, out_hbm,
    hidden, result, gate, up, down, place, unplace,
    outgo, arrive, across, acc_gate, acc_up, acc_logit, partial, partner_part, adj_sum, back, home,
    weight_sem, hidden_sem, out_sem, pass_sem, own_sem,
    out_send, out_recv, x_send, partner_recv, adj_recv, fwd_recv,
    part_send, part_recv, sum_send, sum_recv, home_send, home_recv, home_own,
):
    section = lax.axis_index("section")
    me = lax.axis_index("expert")
    x = lax.rem(me, RING_X)
    zy = me // RING_X
    y = lax.rem(zy, RING_Y)
    z = zy // RING_Y
    partner = x + 1 - 2 * lax.rem(x, 2)
    adjacent = 3 - x
    pair = x // 2
    tok_rows, width = hidden.shape[1], hidden.shape[2]
    chunk = width // CHUNKS
    slots = 4 * PLANE
    partner_id = {"expert": zy * RING_X + partner}
    adjacent_id = {"expert": zy * RING_X + adjacent}

    def peer(i):
        j = i // RING_Y
        dz = jnp.where(lax.rem(j, 2) == 1, (j + 1) // 2, RING_Z - j // 2)
        pz = lax.rem(z + dz, RING_Z)
        py = lax.rem(y + lax.rem(i, RING_Y), RING_Y)
        return pz * RING_Y + py

    weight_copies = [
        pltpu.make_async_copy(gate_hbm.at[0], gate, weight_sem.at[0]),
        pltpu.make_async_copy(up_hbm.at[0], up, weight_sem.at[1]),
        pltpu.make_async_copy(down_hbm.at[0], down, weight_sem.at[2]),
    ]

    @pl.when(section == 0)
    def _():
        for m in range(MB):
            pltpu.make_async_copy(tokens_ref.at[m], hidden.at[m], hidden_sem.at[m]).start()

    for copy in weight_copies:
        copy.start()

    barrier = pltpu.get_barrier_semaphore()

    def greet(i, carry):
        pl.semaphore_signal(
            barrier, inc=1, device_id={"expert": peer(i) * RING_X + x}, device_id_type=MESH
        )
        return carry

    lax.fori_loop(1, PLANE, greet, 0)
    for who in (partner_id, adjacent_id, {"section": 1 - section}):
        pl.semaphore_signal(barrier, inc=1, device_id=who, device_id_type=MESH)

    row_at = lax.broadcasted_iota(jnp.int32, (tok_rows, tok_rows), 0)
    col_at = lax.broadcasted_iota(jnp.int32, (tok_rows, tok_rows), 1)
    for m in range(MB):
        ids_row = ids_ref[pl.ds(m, 1), :]
        ids_mat = jnp.broadcast_to(ids_row, (tok_rows, tok_rows))
        ids_col = jnp.sum(jnp.where(row_at == col_at, ids_mat, 0), axis=1, keepdims=True)
        same = ids_mat == ids_col
        rank_row = jnp.sum(jnp.where(same & (row_at < col_at), 1, 0), axis=0, keepdims=True)
        rank_col = jnp.sum(jnp.where(same & (col_at < row_at), 1, 0), axis=1, keepdims=True)
        target_row = 2 * ids_row + rank_row
        target_col = 2 * ids_col + rank_col
        slot_at = lax.broadcasted_iota(jnp.int32, (slots, tok_rows), 0)
        place[m] = jnp.where(slot_at == target_row, 1.0, 0.0).astype(BF16)
        slot_at = lax.broadcasted_iota(jnp.int32, (tok_rows, slots), 1)
        unplace[m] = jnp.where(slot_at == target_col, 1.0, 0.0).astype(BF16)

    pl.semaphore_wait(barrier, PLANE + 2)

    def dispatch(m):
        landed(hidden.at[m], hidden_sem.at[m])
        wide = hidden[m].astype(F32)
        inv_rms = lax.rsqrt(jnp.mean(wide * wide, axis=-1, keepdims=True) + 1e-06)
        for c in range(CHUNKS):
            span = pl.ds(c * chunk, chunk)
            gain = shared_ref[0:1, span].astype(F32)
            normed = (hidden[m, :, span].astype(F32) * inv_rms * gain).astype(BF16)
            rows = jnp.dot(place[m], normed, preferred_element_type=F32).astype(BF16)
            outgo[m, c] = rows.reshape(PLANE, 2, 2, chunk)
            pltpu.make_async_copy(outgo.at[m, c, zy], arrive.at[m, c, zy], own_sem.at[m, c]).start()

            def send(i, carry):
                to = peer(i)
                pltpu.make_async_remote_copy(
                    src_ref=outgo.at[m, c, to],
                    dst_ref=arrive.at[m, c, zy],
                    send_sem=out_send.at[m, c],
                    recv_sem=out_recv.at[m, c],
                    device_id={"expert": to * RING_X + x},
                    device_id_type=MESH,
                ).start()
                return carry

            lax.fori_loop(1, PLANE, send, 0)

    def x_copy(src, dst, send_sem, recv_sem, who):
        return pltpu.make_async_remote_copy(
            src_ref=src, dst_ref=dst, send_sem=send_sem, recv_sem=recv_sem,
            device_id=who, device_id_type=MESH,
        )

    def to_partner(m, c):
        return x_copy(arrive.at[m, c, :, pair], across.at[m, c, 1], x_send.at[m, c, 0], partner_recv.at[m, c], partner_id)

    def to_adjacent(m, c):
        return x_copy(arrive.at[m, c, :, 1 - pair], across.at[m, c, 0], x_send.at[m, c, 1], adj_recv.at[m, c], adjacent_id)

    def forward(m, c):
        return x_copy(across.at[m, c, 0], across.at[m, c, 2], x_send.at[m, c, 2], fwd_recv.at[m, c], partner_id)

    def part_copy(m, c):
        return x_copy(partial.at[m, c, pl.ds(2, 2)], partner_part.at[m, c], part_send.at[m, c], part_recv.at[m, c], partner_id)

    def sum_copy(m, c):
        return x_copy(adj_sum.at[m, c], back.at[m, c, :, pair], sum_send.at[m, c], sum_recv.at[m, c], adjacent_id)

    def cross(m):
        for c in range(CHUNKS):
            landed(arrive.at[m, c, pl.ds(0, PLANE - 1)], out_recv.at[m, c])
            landed(arrive.at[m, c, 0], own_sem.at[m, c])
            to_adjacent(m, c).start()
            to_partner(m, c).start()
            if c > 0:
                landed(across.at[m, c - 1, 0], adj_recv.at[m, c - 1])
                forward(m, c - 1).start()
        landed(across.at[m, CHUNKS - 1, 0], adj_recv.at[m, CHUNKS - 1])
        forward(m, CHUNKS - 1).start()

    def experts(m):
        if m == 0:
            for copy in weight_copies:
                copy.wait()
        for c in range(CHUNKS):
            landed(across.at[m, c, 1], partner_recv.at[m, c])
            landed(across.at[m, c, 2], fwd_recv.at[m, c])
            span = pl.ds(c * chunk, chunk)
            own = arrive[m, c, :, pl.ds(pair, 1)].reshape(2 * PLANE, chunk)
            rows = jnp.concatenate([own, across[m, c].reshape(6 * PLANE, chunk)], axis=0)
            pre_gate = jnp.dot(rows, gate[span, :], preferred_element_type=F32)
            pre_up = jnp.dot(rows, up[span, :], preferred_element_type=F32)
            column = jnp.broadcast_to(shared_ref[1:2, span], (128, chunk))
            logit = lax.dot_general(rows, column, (((1,), (1,)), ((), ())), preferred_element_type=F32)
            if c == 0:
                acc_gate[...], acc_up[...], acc_logit[...] = pre_gate, pre_up, logit
            else:
                acc_gate[...] += pre_gate
                acc_up[...] += pre_up
                acc_logit[...] += logit
        pre_gate = acc_gate[...]
        activated = (pre_gate / (1.0 + jnp.exp(-pre_gate)) * acc_up[...]).astype(BF16)
        weight = 1.0 / (1.0 + jnp.exp(-acc_logit[:, 0:1]))
        for c in range(CHUNKS):
            span = pl.ds(c * chunk, chunk)
            part = jnp.dot(activated, down[:, span], preferred_element_type=F32) * weight
            partial[m, c] = part.astype(BF16).reshape(4, PLANE, 2, chunk)
            part_copy(m, c).start()

    def reduce(m):
        for c in range(CHUNKS):
            landed(partner_part.at[m, c], part_recv.at[m, c])
            for b in (1, 0):
                mine = partial[m, c, b].reshape(2 * PLANE, chunk).astype(F32)
                other = partner_part[m, c, b].reshape(2 * PLANE, chunk).astype(F32)
                total = (mine + other).astype(BF16).reshape(PLANE, 2, chunk)
                if b == 1:
                    adj_sum[m, c] = total
                    sum_copy(m, c).start()
                else:
                    back[m, c, :, pl.ds(pair, 1)] = total[:, None]

    def give_back(m):
        for c in range(CHUNKS):
            landed(adj_sum.at[m, c], sum_recv.at[m, c])
            pltpu.make_async_copy(back.at[m, c, zy], home.at[m, c, zy], home_own.at[m, c]).start()

            def send(i, carry):
                to = peer(i)
                pltpu.make_async_remote_copy(
                    src_ref=back.at[m, c, to],
                    dst_ref=home.at[m, c, zy],
                    send_sem=home_send.at[m, c],
                    recv_sem=home_recv.at[m, c],
                    device_id={"expert": to * RING_X + x},
                    device_id_type=MESH,
                ).start()
                return carry

            lax.fori_loop(1, PLANE, send, 0)

    def pass_on(m):
        return pltpu.make_async_remote_copy(
            src_ref=result.at[m], dst_ref=hidden.at[m], send_sem=pass_sem.at[m], recv_sem=hidden_sem.at[m],
            device_id={"section": 1}, device_id_type=MESH,
        )

    def combine(m):
        for c in range(CHUNKS):
            landed(home.at[m, c, pl.ds(0, PLANE - 1)], home_recv.at[m, c])
            landed(home.at[m, c, 0], home_own.at[m, c])
            span = pl.ds(c * chunk, chunk)
            spread = jnp.dot(unplace[m], home[m, c].reshape(slots, chunk), preferred_element_type=F32)
            result[m, :, span] = (hidden[m, :, span].astype(F32) + spread).astype(BF16)

        @pl.when(section == 0)
        def _():
            pass_on(m).start()

        pltpu.make_async_copy(result.at[m], out_hbm.at[m], out_sem.at[m]).start()

    dispatch(0)
    dispatch(1)
    for m in range(MB):
        cross(m)
        experts(m)
        reduce(m)
        give_back(m)
    for m in range(MB):
        combine(m)

    for m in range(MB):
        pltpu.make_async_copy(result.at[m], out_hbm.at[m], out_sem.at[m]).wait()

        @pl.when(section == 0)
        def _():
            pass_on(m).wait_send()

        for c in range(CHUNKS):
            landed(outgo.at[m, c, pl.ds(0, PLANE - 1)], out_send.at[m, c])
            landed(back.at[m, c, pl.ds(0, PLANE - 1)], home_send.at[m, c])
            to_partner(m, c).wait_send()
            to_adjacent(m, c).wait_send()
            forward(m, c).wait_send()
            part_copy(m, c).wait_send()
            sum_copy(m, c).wait_send()


def on_device(tokens_in, route_ids, norm_gain, router, gate_proj, up_proj, down_proj):
    devices = lax.axis_size("expert")
    micro_count, tok_rows, width = tokens_in.shape
    units = gate_proj.shape[2]
    share_width = norm_gain.shape[1]
    chunk = width // CHUNKS
    columns = jnp.repeat(router[0].T, HE // units, axis=0)
    gains = jnp.broadcast_to(norm_gain, (devices, share_width))
    spread = jnp.stack([gains, columns], axis=1)
    shared = lax.all_to_all(spread, "expert", split_axis=0, concat_axis=0, tiled=True)
    shared = shared.transpose(1, 0, 2).reshape(2, width)
    ids = route_ids.reshape(micro_count, tok_rows)
    any_space = pl.BlockSpec(memory_space=pl.ANY)
    vmem_space = pl.BlockSpec(memory_space=pltpu.VMEM)
    dma = pltpu.SemaphoreType.DMA
    grid = (MB, CHUNKS)
    out = pl.pallas_call(
        kernel,
        name="routed_experts",
        out_shape=jax.ShapeDtypeStruct((micro_count, tok_rows, width), BF16),
        in_specs=[vmem_space, vmem_space] + [any_space] * 4,
        out_specs=any_space,
        scratch_shapes=[
            pltpu.VMEM((MB, tok_rows, width), BF16),
            pltpu.VMEM((MB, tok_rows, width), BF16),
            pltpu.VMEM((width, units), BF16),
            pltpu.VMEM((width, units), BF16),
            pltpu.VMEM((units, width), BF16),
            pltpu.VMEM((MB, 4 * PLANE, tok_rows), BF16),
            pltpu.VMEM((MB, tok_rows, 4 * PLANE), BF16),
            pltpu.VMEM(grid + (PLANE, 2, 2, chunk), BF16),
            pltpu.VMEM(grid + (PLANE, 2, 2, chunk), BF16),
            pltpu.VMEM(grid + (3, PLANE, 2, chunk), BF16),
            pltpu.VMEM((8 * PLANE, units), F32),
            pltpu.VMEM((8 * PLANE, units), F32),
            pltpu.VMEM((8 * PLANE, 128), F32),
            pltpu.VMEM(grid + (4, PLANE, 2, chunk), BF16),
            pltpu.VMEM(grid + (2, PLANE, 2, chunk), BF16),
            pltpu.VMEM(grid + (PLANE, 2, chunk), BF16),
            pltpu.VMEM(grid + (PLANE, 2, 2, chunk), BF16),
            pltpu.VMEM(grid + (PLANE, 2, 2, chunk), BF16),
            dma((3,)), dma((MB,)), dma((MB,)), dma((MB,)), dma(grid),
            dma(grid), dma(grid), dma(grid + (3,)), dma(grid), dma(grid), dma(grid),
            dma(grid), dma(grid), dma(grid), dma(grid), dma(grid), dma(grid), dma(grid),
        ],
        compiler_params=pltpu.CompilerParams(
            collective_id=0, has_side_effects=True, vmem_limit_bytes=52 * 1024 * 1024
        ),
    )(ids, shared, tokens_in, gate_proj, up_proj, down_proj)
    return out[None]


def solution(mesh):
    return jax.shard_map(
        on_device,
        mesh=mesh,
        in_specs=(
            P(None, "expert", None),
            P("section", None, "expert", None),
            P("section", "expert"),
            P("section", "expert", None),
            P("section", None, "expert"),
            P("section", None, "expert"),
            P("section", "expert", None),
        ),
        out_specs=P("section", None, "expert", None),
        check_vma=False,
    )
```

time: 1150 us -> 208 us (0.18); the launches traced: 1130 us -> 208 us
  blocking collectives: 651 us -> 26.9 us
  waiting for transfers between devices: 295 us -> 0 us
  Pallas kernels: 0 us -> 176 us
  starting transfers between devices: 67.8 us -> 0 us
  matrix products: 49.7 us -> 0 us
  local copies, waits for them, and re-layouts: 51.9 us -> 4.47 us
  other arithmetic: 18.5 us -> 0.02 us
    all_gather x1 -> x0, blocking collectives: 348 us -> none  [on_device(): lax.all_gather(router[0], 'expert', axis=0, tiled=True)]
    unnamed x1 -> x0, blocking collectives: 303 us -> none
    all_to_all x8 -> x0, waiting for transfers between devices: 179 us -> none  [the longest x4 104 us: moe_layer(): lax.all_to_all(copies, 'expert', split_axis=0, concat_axis=0, tiled=True)]
    pallas_call x0 -> x1, Pallas kernels: none -> 176 us  [on_device(): pl.pallas_call(kernel, name='routed_experts', out_shape=jax.ShapeDtypeStr...]
    ppermute x1 -> x0, waiting for transfers between devices: 116 us -> none  [shifted(): return lax.ppermute(block, axis, route)]
    all_to_all x8 -> x0, starting transfers between devices: 66.5 us -> none  [the longest x4 34.5 us: moe_layer(): lax.all_to_all(partial_value, 'expert', split_axis=0, concat_axis=0, tile...]
    dot_general x20 -> x0, matrix products: 49.7 us -> none  [the longest x4 27.5 us: expert_rows(): jnp.dot(activated, down_part, preferred_element_type=jnp.float32)]
    all_to_all x8 -> x0, local copies, waits for them, and re-layouts: 32.2 us -> none  [the longest x4 19 us: moe_layer(): lax.all_to_all(partial_value, 'expert', split_axis=0, concat_axis=0, tile...]
  transfers between devices with their start and end apart: 9 -> 0, of which waited for: 8 -> 0; matrix products, arithmetic and copies ran while one was open for 5% -> 0% of each run, Pallas kernels for 0% -> 0%
where the time goes in v2:
time: 208 us
  Pallas kernels  176 us (85%)
  blocking collectives  26.9 us (13%)
  local copies, waits for them, and re-layouts  4.47 us (2%)
    pallas_call x1, Pallas kernels, on_device(): pl.pallas_call(kernel, name='routed_experts', out_shape=jax.ShapeDtypeStr...  176 us
    all_to_all x1, blocking collectives, on_device(): lax.all_to_all(spread, 'expert', split_axis=0, concat_axis=0, tiled=True)  26.9 us

profile of v2, /device:TPU:1, one launch (start us, length us, event | category | flops | bytes accessed | tf_op | source)
XLA Modules:
  0.0 207.5 jit_solution(6120074542674372391)
XLA Ops:
  0.0 0.8 copy.16
  0.8 0.7 stack_broadcast_in_dim.2
  1.5 0.1 copy.17
  1.6 26.9 %all_to_all.5 = bf16[128,2,28]{2,1,0:T(2,128)(2,1)S(1)} all-to-all(bf16[128,2,28]{2,1,0:T(2,128)(2,1)S(1)} %copy.17), channel_id=1, replica_groups=mesh['section'=2,'expert'=128] {'expert'}, dimensions={0} | all-to-all | bytes 28672 | tf_op jit(solution)/shard_map/all_to_all | solution.py:274
  28.5 0.1 reshape.10.shared_ref
  28.6 0.0 copy-start
  28.6 1.2 copy-done
  29.8 0.0 copy-start.1
  29.8 0.7 copy-done.1
  30.5 176.1 %routed_experts.1 = bf16[2,64,3584]{2,1,0:T(8,128)(2,1)S(1)} custom-call(s32[2,64]{1,0:T(2,128)S(1)} %bitcast.9, bf16[2,3584]{1,0:T(2,128)(2,1)S(1)} %reshape.10.shared_ref, bf16[2,64,3584]{2,1,0:T(8,128)(2,1)S(1)} %copy-done, bf16[1,3584,512]{2,1,0:T(8,128)(2,1)} %gate_hbm.1, bf16[1,3584,512]{2,1,0:T(8,128)(2,1)} %up_hbm.1, bf16[1,512,3584]{2,1,0:T(8,128)(2,1)} %down_hbm.1), custom_call_target="tpu_custom_call" | custom-call | tf_op jit(solution)/shard_map/routed_experts/pallas_call | solution.py:281
  206.6 0.9 copy.20
  (3 shorter events, 0.0 us)
Async XLA Ops:
  28.6 1.2 copy-start
  29.8 0.7 copy-start.1

commit v3 on v2

v3 whole, which is shorter than its diff:
```python
import functools

import jax
import jax.numpy as jnp
from jax import lax
from jax.experimental import pallas as pl
from jax.experimental.pallas import tpu as pltpu
from jax.sharding import PartitionSpec as P

MESH = pl.DeviceIdType.MESH
HE = 1024
MB = 2
RING_X, RING_Y, RING_Z = 4, 4, 8
PLANE = RING_Y * RING_Z
CHUNKS = 4
BF16 = jnp.bfloat16
F32 = jnp.float32
LANES = 128

FIRST = "P0 N00 N01 N02 N03"
SECOND = "P1 N10 N11 N12 N13"
ORDER = (
    "P1a N10a X00 N11a X01 N12a X02 N13a X03 G00 G01 X10a G02 X11a G03 A0 D00 D01 D02 D03 P1b N10b N11b N12b N13b "
    "X10b X11b X12 X13 S00 S01 S02 S03 G10 C00 G11 C01 G12 C02 G13 C03 A1 D10 D11 D12 D13 S10 S11 S12 S13 C10 C11 C12 C13"
)
ALL = tuple(range(CHUNKS))


def parse(names):
    return [(name[0], [int(digit) for digit in name[1:] if digit.isdigit()], name[-1]) for name in names.split()]


def landed(ref, sem):
    pltpu.make_async_copy(ref, ref, sem).wait()


def kernel(
    ids_ref, spread_ref, tokens_ref, gate_hbm, up_hbm, down_hbm, out_hbm,
    hidden, result, scale, gate, up, down, place, unplace, shares, shares_all, shared, selector,
    outgo, arrive, across, acc_gate, acc_up, acc_logit, active, partial, partner_part, back, home,
    weight_sem, hidden_sem, out_sem, pass_sem, own_sem, home_own,
    out_send, out_recv, x_send, x_recv, part_send, part_recv, home_send, home_recv,
    share_send, share_recv, share_x_send, share_x_recv,
):
    section = lax.axis_index("section")
    me = lax.axis_index("expert")
    x = lax.rem(me, RING_X)
    zy = me // RING_X
    y = lax.rem(zy, RING_Y)
    z = zy // RING_Y
    pair = x // 2
    partner = x + 1 - 2 * lax.rem(x, 2)
    adjacent = 3 - x
    far = lax.rem(x + 2, RING_X)
    tok_rows, width = hidden.shape[1], hidden.shape[2]
    chunk = width // CHUNKS
    slots = 4 * PLANE
    across_x = [{"expert": zy * RING_X + q} for q in (adjacent, partner, far)]

    def each_peer(act):
        def plane(j, skip_first):
            dz = jnp.where(lax.rem(j, 2) == 1, (j + 1) // 2, RING_Z - j // 2)
            first = lax.rem(z + dz, RING_Z) * RING_Y
            for dy in range(1 if skip_first else 0, RING_Y):
                act(first + lax.rem(y + dy, RING_Y))

        def body(j, carry):
            plane(j, False)
            return carry

        plane(0, True)
        lax.fori_loop(1, RING_Z, body, 0)

    def remote(src, dst, send_sem, recv_sem, who):
        return pltpu.make_async_remote_copy(
            src_ref=src, dst_ref=dst, send_sem=send_sem, recv_sem=recv_sem,
            device_id=who, device_id_type=MESH,
        )

    def to_plane(src, dst, send_sem, recv_sem, local_sem):
        pltpu.make_async_copy(src.at[zy], dst.at[zy], local_sem).start()

        each_peer(
            lambda to: remote(src.at[to], dst.at[zy], send_sem, recv_sem, {"expert": to * RING_X + x}).start()
        )

    def from_plane(dst, recv_sem, local_sem):
        landed(dst.at[pl.ds(0, PLANE - 1)], recv_sem)
        landed(dst.at[0], local_sem)

    weight_copies = [
        pltpu.make_async_copy(gate_hbm.at[0], gate, weight_sem.at[0]),
        pltpu.make_async_copy(up_hbm.at[0], up, weight_sem.at[1]),
        pltpu.make_async_copy(down_hbm.at[0], down, weight_sem.at[2]),
    ]

    @pl.when(section == 0)
    def _():
        for m in range(MB):
            pltpu.make_async_copy(tokens_ref.at[m], hidden.at[m], hidden_sem.at[m]).start()

    for copy in weight_copies:
        copy.start()

    barrier = pltpu.get_barrier_semaphore()

    each_peer(
        lambda to: pl.semaphore_signal(
            barrier, inc=1, device_id={"expert": to * RING_X + x}, device_id_type=MESH
        )
    )
    for who in across_x + [{"section": 1 - section}]:
        pl.semaphore_signal(barrier, inc=1, device_id=who, device_id_type=MESH)

    row_at = lax.broadcasted_iota(jnp.int32, (tok_rows, tok_rows), 0)
    col_at = lax.broadcasted_iota(jnp.int32, (tok_rows, tok_rows), 1)
    for m in range(MB):
        ids_row = ids_ref[pl.ds(m, 1), :]
        ids_mat = jnp.broadcast_to(ids_row, (tok_rows, tok_rows))
        ids_col = jnp.sum(jnp.where(row_at == col_at, ids_mat, 0), axis=1, keepdims=True)
        same = ids_mat == ids_col
        rank_row = jnp.sum(jnp.where(same & (row_at < col_at), 1, 0), axis=0, keepdims=True)
        rank_col = jnp.sum(jnp.where(same & (col_at < row_at), 1, 0), axis=1, keepdims=True)
        target_row = 2 * ids_row + rank_row
        target_col = 2 * ids_col + rank_col
        slot_at = lax.broadcasted_iota(jnp.int32, (slots, tok_rows), 0)
        place[m] = jnp.where(slot_at == target_row, 1.0, 0.0).astype(BF16)
        slot_at = lax.broadcasted_iota(jnp.int32, (tok_rows, slots), 1)
        unplace[m] = jnp.where(slot_at == target_col, 1.0, 0.0).astype(BF16)

    share_width = width // (RING_X * PLANE)
    column_at = lax.broadcasted_iota(jnp.int32, (1, width), 1)
    column_device = (column_at * ((1 << 18) // share_width + 1)) >> 18
    column_entry = column_at - column_device * share_width
    entry_at = lax.broadcasted_iota(jnp.int32, (LANES, width), 0)
    selector[...] = jnp.where(entry_at == column_entry, 1.0, 0.0).astype(BF16)

    shared[...] = jnp.zeros_like(shared)
    pl.semaphore_wait(barrier, PLANE + 3)
    to_plane(spread_ref, shares, share_send.at[0], share_recv.at[0], share_recv.at[1])

    def x_copies(src_of, dst, send_sems, recv_sem):
        return [remote(src_of(k), dst.at[k], send_sems.at[k], recv_sem, across_x[k]) for k in range(3)]

    share_copies = x_copies(
        lambda k: shares.at[:, pair if k == 1 else 1 - pair], shares_all.at[pl.ds(1, 3)], share_x_send, share_x_recv.at[0]
    )

    def pass_shares():
        from_plane(shares, share_recv.at[0], share_recv.at[1])
        for copy in share_copies:
            copy.start()
        shares_all[0] = shares[:, pl.ds(pair, 1)].reshape(PLANE, 2, LANES)

    def collect_shares():
        landed(shares_all.at[pl.ds(1, 3)], share_x_recv.at[0])
        blocks = shares_all[...].reshape(8 * PLANE, LANES)
        row = lax.broadcasted_iota(jnp.int32, (8 * PLANE, 1), 0)
        block = row // (2 * PLANE)
        row_x = jnp.where(block == 0, x, jnp.where(block == 1, adjacent, jnp.where(block == 2, partner, far)))
        row_device = lax.rem(row // 2, PLANE) * RING_X + row_x
        kind = lax.rem(lax.broadcasted_iota(jnp.int32, (8, 8 * PLANE), 1), 2)
        kinds = jnp.where(kind == lax.broadcasted_iota(jnp.int32, (8, 8 * PLANE), 0), 1.0, 0.0).astype(BF16)
        for c in ALL:
            span = pl.ds(c * chunk, chunk)
            entries = jnp.dot(blocks, selector[:, span], preferred_element_type=F32)
            device_of = (
                (lax.broadcasted_iota(jnp.int32, (1, chunk), 1) + c * chunk) * ((1 << 18) // share_width + 1)
            ) >> 18
            picked = jnp.where(row_device == device_of, entries, 0.0).astype(BF16)
            shared[:, span] = jnp.dot(kinds, picked, preferred_element_type=F32)

    def expert_gain(span):
        return jnp.where(section == 0, shared[0:1, span], 1.0).astype(BF16)

    def step_p(m):
        landed(hidden.at[m], hidden_sem.at[m])
        wide = hidden[m].astype(F32)
        inv_rms = lax.rsqrt(jnp.mean(wide * wide, axis=-1, keepdims=True) + 1e-06)
        scale[m] = jnp.broadcast_to(inv_rms, (tok_rows, LANES))

    def step_n(m, c, gained=True):
        span = pl.ds(c * chunk, chunk)
        normed = hidden[m, :, span].astype(F32) * scale[m, :, 0:1]
        if gained:
            normed = normed * shared[0:1, span]
        rows = jnp.dot(place[m], normed.astype(BF16), preferred_element_type=F32).astype(BF16)
        outgo[m, c] = rows.reshape(PLANE, 2, 2, chunk)
        to_plane(outgo.at[m, c], arrive.at[m, c], out_send.at[m, c], out_recv.at[m, c], own_sem.at[m, c])

    def share_rows(m, c):
        return x_copies(
            lambda k: arrive.at[m, c, :, pair if k == 1 else 1 - pair], across.at[m, c], x_send.at[m, c], x_recv.at[m, c]
        )

    def step_x(m, c):
        from_plane(arrive.at[m, c], out_recv.at[m, c], own_sem.at[m, c])
        for copy in share_rows(m, c):
            copy.start()

    def step_g(m, c):
        if m == 0 and c == 0:
            weight_copies[0].wait()
            weight_copies[1].wait()
        landed(across.at[m, c], x_recv.at[m, c])
        span = pl.ds(c * chunk, chunk)
        own = arrive[m, c, :, pl.ds(pair, 1)].reshape(2 * PLANE, chunk)
        rows = jnp.concatenate([own, across[m, c].reshape(6 * PLANE, chunk)], axis=0)
        rows = rows * expert_gain(span)
        pre_gate = jnp.dot(rows, gate[span, :], preferred_element_type=F32)
        pre_up = jnp.dot(rows, up[span, :], preferred_element_type=F32)
        column = jnp.broadcast_to(shared[1:2, span], (LANES, chunk)).astype(BF16)
        logit = lax.dot_general(rows, column, (((1,), (1,)), ((), ())), preferred_element_type=F32)
        if c == 0:
            acc_gate[...], acc_up[...], acc_logit[...] = pre_gate, pre_up, logit
        else:
            acc_gate[...] += pre_gate
            acc_up[...] += pre_up
            acc_logit[...] += logit

    def step_a(m):
        pre_gate = acc_gate[...]
        active[...] = (pre_gate / (1.0 + jnp.exp(-pre_gate)) * acc_up[...]).astype(BF16)
        if m == 0:
            weight_copies[2].wait()

    def part_copies(m, c):
        return [
            remote(partial.at[m, c, k + 1], partner_part.at[m, c, k], part_send.at[m, c, k], part_recv.at[m, c], across_x[k])
            for k in range(3)
        ]

    def step_d(m, c):
        weight = 1.0 / (1.0 + jnp.exp(-acc_logit[:, 0:1]))
        part = jnp.dot(active[...], down[:, pl.ds(c * chunk, chunk)], preferred_element_type=F32) * weight
        partial[m, c] = part.astype(BF16).reshape(4, PLANE, 2, chunk)
        for copy in part_copies(m, c):
            copy.start()

    def step_s(m, c):
        landed(partner_part.at[m, c], part_recv.at[m, c])

        def rows_of(ref):
            return ref[...].reshape(2 * PLANE, chunk).astype(F32)

        own = rows_of(partial.at[m, c, 0]) + rows_of(partner_part.at[m, c, 1])
        other = rows_of(partner_part.at[m, c, 0]) + rows_of(partner_part.at[m, c, 2])
        back[m, c, :, pl.ds(pair, 1)] = own.astype(BF16).reshape(PLANE, 1, 2, chunk)
        back[m, c, :, pl.ds(1 - pair, 1)] = other.astype(BF16).reshape(PLANE, 1, 2, chunk)
        to_plane(back.at[m, c], home.at[m, c], home_send.at[m, c], home_recv.at[m, c], home_own.at[m, c])

    def pass_on(m, c):
        piece = (m, slice(None), pl.ds(c * chunk, chunk))
        return remote(result.at[piece], hidden.at[piece], pass_sem.at[m], hidden_sem.at[m], {"section": 1})

    def out_copy(m, c):
        piece = (m, slice(None), pl.ds(c * chunk, chunk))
        return pltpu.make_async_copy(result.at[piece], out_hbm.at[piece], out_sem.at[m, c])

    def step_c(m, c):
        from_plane(home.at[m, c], home_recv.at[m, c], home_own.at[m, c])
        span = pl.ds(c * chunk, chunk)
        spread = jnp.dot(unplace[m], home[m, c].reshape(slots, chunk), preferred_element_type=F32)
        result[m, :, span] = (hidden[m, :, span].astype(F32) + spread).astype(BF16)
        pl.when(section == 0)(lambda: pass_on(m, c).start())
        out_copy(m, c).start()

    steps = dict(P=step_p, N=step_n, X=step_x, G=step_g, A=step_a, D=step_d, S=step_s, C=step_c)

    def run(names, **kind):
        for letter, numbers, only in parse(names):
            extra = {}
            if letter == "N":
                extra = dict(gained=False) if only == "a" else kind
            step = functools.partial(steps[letter], *numbers, **extra)
            if only in "ab":
                pl.when(section == "ab".index(only))(step)
            else:
                step()

    pl.when(section == 0)(lambda: run(FIRST, gained=False))
    pass_shares()

    @pl.when(section == 1)
    def _():
        collect_shares()
        run(FIRST)

    before, after = ORDER.split(" G00 ")
    run(before)
    pl.when(section == 0)(collect_shares)
    run("G00 " + after)

    landed(shares.at[pl.ds(0, PLANE - 1)], share_send.at[0])
    for copy in share_copies:
        copy.wait_send()
    for m in range(MB):
        pl.when(section == 0)(functools.partial(landed, result.at[m], pass_sem.at[m]))
        for c in ALL:
            landed(outgo.at[m, c, pl.ds(0, PLANE - 1)], out_send.at[m, c])
            for copy in share_rows(m, c) + part_copies(m, c):
                copy.wait_send()
            landed(back.at[m, c, pl.ds(0, PLANE - 1)], home_send.at[m, c])
            out_copy(m, c).wait()


def on_device(tokens_in, route_ids, norm_gain, router, gate_proj, up_proj, down_proj):
    micro_count, tok_rows, width = tokens_in.shape
    units = gate_proj.shape[2]
    share_width = norm_gain.shape[1]
    chunk = width // CHUNKS
    columns = router[0].T.reshape(PLANE, 2, 1, share_width)
    gains = jnp.broadcast_to(norm_gain, columns.shape)
    spread = jnp.pad(jnp.concatenate([gains, columns], axis=2), ((0, 0), (0, 0), (0, 0), (0, LANES - share_width)))
    ids = route_ids.reshape(micro_count, tok_rows)
    any_space = pl.BlockSpec(memory_space=pl.ANY)
    vmem_space = pl.BlockSpec(memory_space=pltpu.VMEM)
    dma = pltpu.SemaphoreType.DMA
    grid = (MB, CHUNKS)
    out = pl.pallas_call(
        kernel,
        name="routed_experts",
        out_shape=jax.ShapeDtypeStruct((micro_count, tok_rows, width), BF16),
        in_specs=[vmem_space, vmem_space] + [any_space] * 4,
        out_specs=any_space,
        scratch_shapes=[
            pltpu.VMEM((MB, tok_rows, width), BF16),
            pltpu.VMEM((MB, tok_rows, width), BF16),
            pltpu.VMEM((MB, tok_rows, LANES), F32),
            pltpu.VMEM((width, units), BF16),
            pltpu.VMEM((width, units), BF16),
            pltpu.VMEM((units, width), BF16),
            pltpu.VMEM((MB, 4 * PLANE, tok_rows), BF16),
            pltpu.VMEM((MB, tok_rows, 4 * PLANE), BF16),
            pltpu.VMEM((PLANE, 2, 2, LANES), BF16),
            pltpu.VMEM((4, PLANE, 2, LANES), BF16),
            pltpu.VMEM((8, width), F32),
            pltpu.VMEM((LANES, width), BF16),
            pltpu.VMEM(grid + (PLANE, 2, 2, chunk), BF16),
            pltpu.VMEM(grid + (PLANE, 2, 2, chunk), BF16),
            pltpu.VMEM(grid + (3, PLANE, 2, chunk), BF16),
            pltpu.VMEM((8 * PLANE, units), F32),
            pltpu.VMEM((8 * PLANE, units), F32),
            pltpu.VMEM((8 * PLANE, LANES), F32),
            pltpu.VMEM((8 * PLANE, units), BF16),
            pltpu.VMEM(grid + (4, PLANE, 2, chunk), BF16),
            pltpu.VMEM(grid + (3, PLANE, 2, chunk), BF16),
            pltpu.VMEM(grid + (PLANE, 2, 2, chunk), BF16),
            pltpu.VMEM(grid + (PLANE, 2, 2, chunk), BF16),
            dma((3,)), dma((MB,)), dma(grid), dma((MB,)), dma(grid), dma(grid),
            dma(grid), dma(grid), dma(grid + (3,)), dma(grid), dma(grid + (3,)), dma(grid), dma(grid), dma(grid),
            dma((1,)), dma((2,)), dma((3,)), dma((1,)),
        ],
        compiler_params=pltpu.CompilerParams(
            collective_id=0, has_side_effects=True, vmem_limit_bytes=52 * 1024 * 1024
        ),
    )(ids, spread, tokens_in, gate_proj, up_proj, down_proj)
    return out[None]


def solution(mesh):
    return jax.shard_map(
        on_device,
        mesh=mesh,
        in_specs=(
            P(None, "expert", None),
            P("section", None, "expert", None),
            P("section", "expert"),
            P("section", "expert", None),
            P("section", None, "expert"),
            P("section", None, "expert"),
            P("section", "expert", None),
        ),
        out_specs=P("section", None, "expert", None),
        check_vma=False,
    )
```

time: 208 us -> 144 us (0.69)
  Pallas kernels: 176 us -> 140 us
  blocking collectives: 26.9 us -> 0 us
    pallas_call x1, Pallas kernels: 176 us -> 140 us  [on_device(): pl.pallas_call(kernel, name='routed_experts', out_shape=jax.ShapeDtypeStr...]
    all_to_all x1 -> x0, blocking collectives: 26.9 us -> none  [on_device(): lax.all_to_all(spread, 'expert', split_axis=0, concat_axis=0, tiled=True)]
where the time goes in v3:
time: 144 us
  Pallas kernels  140 us (97%)
  local copies, waits for them, and re-layouts  4.28 us (3%)
    pallas_call x1, Pallas kernels, on_device(): pl.pallas_call(kernel, name='routed_experts', out_shape=jax.ShapeDtypeStr...  140 us

profile of v3, /device:TPU:1, one launch (start us, length us, event | category | flops | bytes accessed | tf_op | source)
XLA Modules:
  0.0 144.2 jit_solution(11707514378503892136)
XLA Ops:
  0.0 0.8 copy.9
  0.8 0.7 broadcast_in_dim.6
  1.5 0.1 fusion.2.spread_ref
  1.6 0.0 copy-start
  1.6 1.2 copy-done
  2.8 0.0 copy-start.1
  2.8 0.7 copy-done.1
  3.5 139.8 %routed_experts.1 = bf16[2,64,3584]{2,1,0:T(8,128)(2,1)S(1)} custom-call(s32[2,64]{1,0:T(2,128)S(1)} %bitcast.8, bf16[32,2,2,128]{3,2,1,0:T(2,128)(2,1)S(1)} %fusion.2.spread_ref, bf16[2,64,3584]{2,1,0:T(8,128)(2,1)S(1)} %copy-done, bf16[1,3584,512]{2,1,0:T(8,128)(2,1)} %gate_hbm.1, bf16[1,3584,512]{2,1,0:T(8,128)(2,1)} %up_hbm.1, bf16[1,512,3584]{2,1,0:T(8,128)(2,1)} %down_hbm.1), custom_call_target="tpu_custom_call" | custom-call | tf_op jit(solution)/shard_map/routed_experts/pallas_call | solution.py:320
  143.3 0.9 copy.12
  (1 shorter events, 0.0 us)
Async XLA Ops:
  1.6 1.2 copy-start
  2.8 0.7 copy-start.1

commit v4 on v3

v4 whole, which is shorter than its diff:
```python
import functools

import jax
import jax.numpy as jnp
from jax import lax
from jax.experimental import pallas as pl
from jax.experimental.pallas import tpu as pltpu
from jax.sharding import PartitionSpec as P

MESH = pl.DeviceIdType.MESH
HE = 1024
MB = 2
RING_X, RING_Y, RING_Z = 4, 4, 8
PLANE = RING_Y * RING_Z
CHUNKS = 2
BF16 = jnp.bfloat16
F32 = jnp.float32
LANES = 128

ALL = tuple(range(CHUNKS))
HALVES = (0, 1)
HALF = PLANE // 2
OWN = HALF - RING_Y
FIRST = ("N00a", "N01a", "M00a", "M01a")
ORDER = (
    "N00b", "M00b", "N01b", "M01b", "N10a", "N11a", "X000", "M10a", "X001a", "M11a", "X010", "X001b",
    "G000", "G010b", "G001", "A00", "X011", "D000", "D001", "G010a", "G011", "A01", "D010", "D011",
    "N10b", "M10b", "N11b", "M11b", "X100", "X110b", "X101", "X110a", "X111", "S000", "S001", "S010", "S011",
    "G100", "G101", "A10", "D100", "D101", "C00", "C01", "G110", "G111", "A11", "D110", "D111",
    "S100", "S101", "S110", "S111", "C10", "C11",
)


def parse(names):
    return [(name[0], [int(digit) for digit in name[1:] if digit.isdigit()], name[-1]) for name in names]


def landed(ref, sem):
    pltpu.make_async_copy(ref, ref, sem).wait()


def kernel(
    ids_hbm, spread_hbm, tokens_ref, gate_hbm, up_hbm, down_hbm, out_hbm,
    ids_ref, spread_ref, hidden, result, gate, up, down, place, unplace, shares, shares_all, shared, selector,
    outgo, arrive, across, acc_gate, acc_up, acc_logit, acc_square, weight, active, partial, partner_part, back, home,
    small_sem, weight_sem, hidden_sem, out_sem, pass_sem, own_sem, home_own,
    out_send, out_recv, x_send, x_recv, part_send, part_recv, home_send, home_recv,
    share_send, share_recv, share_x_send, share_x_recv,
):
    section = lax.axis_index("section")
    me = lax.axis_index("expert")
    x = lax.rem(me, RING_X)
    zy = me // RING_X
    y = lax.rem(zy, RING_Y)
    z = zy // RING_Y
    pair = x // 2
    partner = x + 1 - 2 * lax.rem(x, 2)
    adjacent = 3 - x
    far = lax.rem(x + 2, RING_X)
    tok_rows, width = hidden.shape[1], hidden.shape[2]
    chunk = width // CHUNKS
    slots = 4 * PLANE
    across_x = [{"expert": zy * RING_X + q} for q in (adjacent, partner, far)]

    def each_peer(half, act):
        def plane(k, dz, first):
            for dy in range(first, RING_Y):
                there = lax.rem(z + dz, RING_Z) * RING_Y + lax.rem(y + dy, RING_Y)
                thence = lax.rem(z + RING_Z - dz, RING_Z) * RING_Y + lax.rem(y + RING_Y - dy, RING_Y)
                act(k * RING_Y + dy, there, thence)

        def body(k, carry):
            plane(k, 2 * k + 2 - half, 0)
            return carry

        lax.fori_loop(0, RING_Z // 2 - 1 + half, body, 0)
        if half == 0:
            plane(RING_Z // 2 - 1, 0, 1)

    def remote(src, dst, send_sem, recv_sem, who):
        return pltpu.make_async_remote_copy(
            src_ref=src, dst_ref=dst, send_sem=send_sem, recv_sem=recv_sem,
            device_id=who, device_id_type=MESH,
        )

    def at_x(there):
        return {"expert": there * RING_X + x}

    def half_landed(dst, half, recv_sem, local_sem):
        landed(dst.at[pl.ds(0, HALF - 1 + half)], recv_sem)
        if half == 0:
            landed(dst.at[0], local_sem)

    weight_copies = [
        pltpu.make_async_copy(gate_hbm.at[0], gate, weight_sem.at[0]),
        pltpu.make_async_copy(up_hbm.at[0], up, weight_sem.at[1]),
        pltpu.make_async_copy(down_hbm.at[0], down, weight_sem.at[2]),
    ]

    ids_copy = pltpu.make_async_copy(ids_hbm, ids_ref, small_sem.at[0])
    spread_copy = pltpu.make_async_copy(spread_hbm, spread_ref, small_sem.at[1])
    ids_copy.start()
    spread_copy.start()

    @pl.when(section == 0)
    def _():
        for m in range(MB):
            for c in ALL:
                piece = (m, slice(None), pl.ds(c * chunk, chunk))
                pltpu.make_async_copy(tokens_ref.at[piece], hidden.at[piece], hidden_sem.at[m, c]).start()

    for copy in weight_copies:
        copy.start()

    barrier = pltpu.get_barrier_semaphore()

    for half in HALVES:
        each_peer(
            half,
            lambda i, there, thence: pl.semaphore_signal(
                barrier, inc=1, device_id=at_x(there), device_id_type=MESH
            ),
        )
    for who in across_x + [{"section": 1 - section}]:
        pl.semaphore_signal(barrier, inc=1, device_id=who, device_id_type=MESH)

    ids_copy.wait()
    row_at = lax.broadcasted_iota(jnp.int32, (tok_rows, tok_rows), 0)
    col_at = lax.broadcasted_iota(jnp.int32, (tok_rows, tok_rows), 1)
    for m in range(MB):
        ids_row = ids_ref[pl.ds(m, 1), :]
        ids_mat = jnp.broadcast_to(ids_row, (tok_rows, tok_rows))
        ids_col = jnp.sum(jnp.where(row_at == col_at, ids_mat, 0), axis=1, keepdims=True)
        same = ids_mat == ids_col
        rank_row = jnp.sum(jnp.where(same & (row_at < col_at), 1, 0), axis=0, keepdims=True)
        rank_col = jnp.sum(jnp.where(same & (col_at < row_at), 1, 0), axis=1, keepdims=True)
        target_row = 2 * ids_row + rank_row
        target_col = 2 * ids_col + rank_col
        slot_at = lax.broadcasted_iota(jnp.int32, (slots, tok_rows), 0)
        place[m] = jnp.where(slot_at == target_row, 1.0, 0.0).astype(BF16)
        slot_at = lax.broadcasted_iota(jnp.int32, (tok_rows, slots), 1)
        unplace[m] = jnp.where(slot_at == target_col, 1.0, 0.0).astype(BF16)

    share_width = width // (RING_X * PLANE)
    column_at = lax.broadcasted_iota(jnp.int32, (1, width), 1)
    column_device = (column_at * ((1 << 18) // share_width + 1)) >> 18
    column_entry = column_at - column_device * share_width
    entry_at = lax.broadcasted_iota(jnp.int32, (LANES, width), 0)
    selector[...] = jnp.where(entry_at == column_entry, 1.0, 0.0).astype(BF16)

    shared[...] = jnp.zeros_like(shared)
    pl.semaphore_wait(barrier, PLANE + 3)
    spread_copy.wait()
    shares[pl.ds(zy, 1)] = spread_ref[pl.ds(zy, 1)]
    for half in HALVES:
        each_peer(
            half,
            lambda i, there, thence: remote(
                spread_ref.at[there], shares.at[zy], share_send.at[0], share_recv.at[0], at_x(there)
            ).start(),
        )

    def x_copies(src_of, dst, send_sems, recv_sem):
        return [remote(src_of(k), dst.at[k], send_sems.at[k], recv_sem, across_x[k]) for k in range(3)]

    share_copies = x_copies(
        lambda k: shares.at[:, pair if k == 1 else 1 - pair], shares_all.at[pl.ds(1, 3)], share_x_send, share_x_recv.at[0]
    )

    def pass_shares():
        landed(shares.at[pl.ds(0, PLANE - 1)], share_recv.at[0])
        for copy in share_copies:
            copy.start()
        shares_all[0] = shares[:, pl.ds(pair, 1)].reshape(PLANE, 2, LANES)

    def collect_shares():
        landed(shares_all.at[pl.ds(1, 3)], share_x_recv.at[0])
        blocks = shares_all[...].reshape(8 * PLANE, LANES)
        row = lax.broadcasted_iota(jnp.int32, (8 * PLANE, 1), 0)
        block = row // (2 * PLANE)
        row_x = jnp.where(block == 0, x, jnp.where(block == 1, adjacent, jnp.where(block == 2, partner, far)))
        row_device = lax.rem(row // 2, PLANE) * RING_X + row_x
        kind = lax.rem(lax.broadcasted_iota(jnp.int32, (8, 8 * PLANE), 1), 2)
        kinds = jnp.where(kind == lax.broadcasted_iota(jnp.int32, (8, 8 * PLANE), 0), 1.0, 0.0).astype(BF16)
        for c in ALL:
            span = pl.ds(c * chunk, chunk)
            entries = jnp.dot(blocks, selector[:, span], preferred_element_type=F32)
            device_of = (
                (lax.broadcasted_iota(jnp.int32, (1, chunk), 1) + c * chunk) * ((1 << 18) // share_width + 1)
            ) >> 18
            picked = jnp.where(row_device == device_of, entries, 0.0).astype(BF16)
            shared[:, span] = jnp.dot(kinds, picked, preferred_element_type=F32)

    def step_n(m, c):
        span = pl.ds(c * chunk, chunk)
        landed(hidden.at[m, :, span], hidden_sem.at[m, c])
        rows = jnp.dot(place[m], hidden[m, :, span], preferred_element_type=F32).astype(BF16)
        outgo[m, c] = rows.reshape(PLANE, 2, 2, chunk)
        pltpu.make_async_copy(outgo.at[m, c, zy], arrive.at[m, 0, c, OWN], own_sem.at[m, c]).start()
        send_half(m, 0, c)

    def send_half(m, half, c):
        each_peer(
            half,
            lambda i, there, thence: remote(
                outgo.at[m, c, there], arrive.at[m, half, c, i], out_send.at[m, c], out_recv.at[m, half, c], at_x(there)
            ).start(),
        )

    def step_m(m, c):
        send_half(m, 1, c)

    def share_rows(m, half, c):
        return x_copies(
            lambda k: arrive.at[m, half, c, :, pair if k == 1 else 1 - pair],
            across.at[m, half, c], x_send.at[m, half, c], x_recv.at[m, half, c],
        )

    def step_x(m, half, c):
        half_landed(arrive.at[m, half, c], half, out_recv.at[m, half, c], own_sem.at[m, c])
        for copy in share_rows(m, half, c):
            copy.start()

    def step_g(m, half, c):
        if (m, half, c) == (0, 0, 0):
            weight_copies[0].wait()
            weight_copies[1].wait()
        landed(across.at[m, half, c], x_recv.at[m, half, c])
        span = pl.ds(c * chunk, chunk)
        own = arrive[m, half, c, :, pl.ds(pair, 1)].reshape(2 * HALF, chunk)
        rows = jnp.concatenate([own, across[m, half, c].reshape(6 * HALF, chunk)], axis=0)
        square = jnp.zeros((8 * HALF, LANES), F32)
        for lane in range(0, chunk, LANES):
            piece = rows[:, lane:lane + LANES].astype(F32)
            square += piece * piece
        rows = rows * shared[0:1, span].astype(BF16)
        pre_gate = jnp.dot(rows, gate[span, :], preferred_element_type=F32)
        pre_up = jnp.dot(rows, up[span, :], preferred_element_type=F32)
        column = jnp.broadcast_to(shared[1:2, span], (LANES, chunk)).astype(BF16)
        logit = lax.dot_general(rows, column, (((1,), (1,)), ((), ())), preferred_element_type=F32)
        if c == 0:
            acc_gate[half], acc_up[half], acc_logit[half], acc_square[half] = pre_gate, pre_up, logit, square
        else:
            acc_gate[half] += pre_gate
            acc_up[half] += pre_up
            acc_logit[half] += logit
            acc_square[half] += square

    def step_a(m, half):
        inv_rms = lax.rsqrt(jnp.sum(acc_square[half], axis=1, keepdims=True) * (1.0 / width) + 1e-06)
        pre_gate = acc_gate[half] * inv_rms
        active[half] = (pre_gate / (1.0 + jnp.exp(-pre_gate)) * (acc_up[half] * inv_rms)).astype(BF16)
        weight[half] = 1.0 / (1.0 + jnp.exp(-acc_logit[half] * inv_rms))
        if (m, half) == (0, 0):
            weight_copies[2].wait()

    def part_copies(m, half, c):
        return [
            remote(
                partial.at[m, half, c, k + 1], partner_part.at[m, half, c, k],
                part_send.at[m, half, c, k], part_recv.at[m, half, c], across_x[k],
            )
            for k in range(3)
        ]

    def step_d(m, half, c):
        part = jnp.dot(active[half], down[:, pl.ds(c * chunk, chunk)], preferred_element_type=F32) * weight[half, :, 0:1]
        partial[m, half, c] = part.astype(BF16).reshape(4, HALF, 2, chunk)
        for copy in part_copies(m, half, c):
            copy.start()

    def step_s(m, half, c):
        landed(partner_part.at[m, half, c], part_recv.at[m, half, c])

        def rows_of(ref):
            return ref[...].reshape(2 * HALF, chunk).astype(F32)

        own = rows_of(partial.at[m, half, c, 0]) + rows_of(partner_part.at[m, half, c, 1])
        other = rows_of(partner_part.at[m, half, c, 0]) + rows_of(partner_part.at[m, half, c, 2])
        back[m, half, c, :, pl.ds(pair, 1)] = own.astype(BF16).reshape(HALF, 1, 2, chunk)
        back[m, half, c, :, pl.ds(1 - pair, 1)] = other.astype(BF16).reshape(HALF, 1, 2, chunk)
        if half == 0:
            pltpu.make_async_copy(back.at[m, 0, c, OWN], home.at[m, c, zy], home_own.at[m, c]).start()
        each_peer(
            half,
            lambda i, there, thence: remote(
                back.at[m, half, c, i], home.at[m, c, zy], home_send.at[m, half, c], home_recv.at[m, half, c], at_x(thence)
            ).start(),
        )

    def pass_on(m, c):
        piece = (m, slice(None), pl.ds(c * chunk, chunk))
        return remote(result.at[piece], hidden.at[piece], pass_sem.at[m], hidden_sem.at[m, c], {"section": 1})

    def out_copy(m, c):
        piece = (m, slice(None), pl.ds(c * chunk, chunk))
        return pltpu.make_async_copy(result.at[piece], out_hbm.at[piece], out_sem.at[m, c])

    def step_c(m, c):
        for half in HALVES:
            half_landed(home.at[m, c], half, home_recv.at[m, half, c], home_own.at[m, c])
        span = pl.ds(c * chunk, chunk)
        spread = jnp.dot(unplace[m], home[m, c].reshape(slots, chunk), preferred_element_type=F32)
        result[m, :, span] = (hidden[m, :, span].astype(F32) + spread).astype(BF16)
        pl.when(section == 0)(lambda: pass_on(m, c).start())
        out_copy(m, c).start()

    steps = dict(N=step_n, M=step_m, X=step_x, G=step_g, A=step_a, D=step_d, S=step_s, C=step_c)

    def run(names):
        for letter, numbers, only in parse(names):
            step = functools.partial(steps[letter], *numbers)
            if only in "ab":
                pl.when(section == "ab".index(only))(step)
            else:
                step()

    begin = ORDER.index("G000")
    run(FIRST)
    pass_shares()
    run(ORDER[:begin])
    collect_shares()
    run(ORDER[begin:])

    landed(shares.at[pl.ds(0, PLANE - 1)], share_send.at[0])
    for copy in share_copies:
        copy.wait_send()
    for m in range(MB):
        pl.when(section == 0)(functools.partial(landed, result.at[m], pass_sem.at[m]))
        for c in ALL:
            landed(outgo.at[m, c, pl.ds(0, PLANE - 1)], out_send.at[m, c])
            for half in HALVES:
                for copy in share_rows(m, half, c) + part_copies(m, half, c):
                    copy.wait_send()
                landed(back.at[m, half, c, pl.ds(0, HALF - 1 + half)], home_send.at[m, half, c])
            out_copy(m, c).wait()


def on_device(tokens_in, route_ids, norm_gain, router, gate_proj, up_proj, down_proj):
    micro_count, tok_rows, width = tokens_in.shape
    units = gate_proj.shape[2]
    share_width = norm_gain.shape[1]
    chunk = width // CHUNKS
    columns = router[0].T.reshape(PLANE, 2, 1, share_width)
    gains = jnp.broadcast_to(norm_gain, columns.shape)
    spread = jnp.pad(jnp.concatenate([gains, columns], axis=2), ((0, 0), (0, 0), (0, 0), (0, LANES - share_width)))
    ids = route_ids.reshape(micro_count, tok_rows)
    any_space = pl.BlockSpec(memory_space=pl.ANY)
    dma = pltpu.SemaphoreType.DMA
    grid = (MB, 2, CHUNKS)
    out = pl.pallas_call(
        kernel,
        name="routed_experts",
        out_shape=jax.ShapeDtypeStruct((micro_count, tok_rows, width), BF16),
        in_specs=[any_space] * 6,
        out_specs=any_space,
        scratch_shapes=[
            pltpu.VMEM((MB, tok_rows), jnp.int32),
            pltpu.VMEM((PLANE, 2, 2, LANES), BF16),
            pltpu.VMEM((MB, tok_rows, width), BF16),
            pltpu.VMEM((MB, tok_rows, width), BF16),
            pltpu.VMEM((width, units), BF16),
            pltpu.VMEM((width, units), BF16),
            pltpu.VMEM((units, width), BF16),
            pltpu.VMEM((MB, 4 * PLANE, tok_rows), BF16),
            pltpu.VMEM((MB, tok_rows, 4 * PLANE), BF16),
            pltpu.VMEM((PLANE, 2, 2, LANES), BF16),
            pltpu.VMEM((4, PLANE, 2, LANES), BF16),
            pltpu.VMEM((8, width), F32),
            pltpu.VMEM((LANES, width), BF16),
            pltpu.VMEM((MB, CHUNKS, PLANE, 2, 2, chunk), BF16),
            pltpu.VMEM(grid + (HALF, 2, 2, chunk), BF16),
            pltpu.VMEM(grid + (3, HALF, 2, chunk), BF16),
            pltpu.VMEM((2, 8 * HALF, units), F32),
            pltpu.VMEM((2, 8 * HALF, units), F32),
            pltpu.VMEM((2, 8 * HALF, LANES), F32),
            pltpu.VMEM((2, 8 * HALF, LANES), F32),
            pltpu.VMEM((2, 8 * HALF, LANES), F32),
            pltpu.VMEM((2, 8 * HALF, units), BF16),
            pltpu.VMEM(grid + (4, HALF, 2, chunk), BF16),
            pltpu.VMEM(grid + (3, HALF, 2, chunk), BF16),
            pltpu.VMEM(grid + (HALF, 2, 2, chunk), BF16),
            pltpu.VMEM((MB, CHUNKS, PLANE, 2, 2, chunk), BF16),
            dma((2,)), dma((3,)), dma((MB, CHUNKS)), dma((MB, CHUNKS)), dma((MB,)), dma((MB, CHUNKS)), dma((MB, CHUNKS)),
            dma((MB, CHUNKS)), dma(grid), dma(grid + (3,)), dma(grid), dma(grid + (3,)), dma(grid), dma(grid), dma(grid),
            dma((1,)), dma((1,)), dma((3,)), dma((1,)),
        ],
        compiler_params=pltpu.CompilerParams(
            collective_id=0, has_side_effects=True, vmem_limit_bytes=52 * 1024 * 1024
        ),
    )(ids, spread, tokens_in, gate_proj, up_proj, down_proj)
    return out[None]


def solution(mesh):
    return jax.shard_map(
        on_device,
        mesh=mesh,
        in_specs=(
            P(None, "expert", None),
            P("section", None, "expert", None),
            P("section", "expert"),
            P("section", "expert", None),
            P("section", None, "expert"),
            P("section", None, "expert"),
            P("section", "expert", None),
        ),
        out_specs=P("section", None, "expert", None),
        check_vma=False,
    )
```

time: 144 us -> 132 us (0.917)
  Pallas kernels: 140 us -> 127 us
    pallas_call x1, Pallas kernels: 140 us -> 127 us  [on_device(): pl.pallas_call(kernel, name='routed_experts', out_shape=jax.ShapeDtypeStr...]
where the time goes in v4:
time: 132 us
  Pallas kernels  127 us (96%)
  local copies, waits for them, and re-layouts  4.28 us (3%)
    pallas_call x1, Pallas kernels, on_device(): pl.pallas_call(kernel, name='routed_experts', out_shape=jax.ShapeDtypeStr...  127 us
    unnamed x5, local copies, waits for them, and re-layouts  2.78 us

profile of v4, /device:TPU:1, one launch (start us, length us, event | category | flops | bytes accessed | tf_op | source)
XLA Modules:
  0.0 131.9 jit_solution(3678079181965236146)
XLA Ops:
  0.0 0.8 copy.9
  0.8 0.7 broadcast_in_dim.6
  1.5 0.1 fusion.2.spread_hbm
  1.6 0.0 copy-start
  1.6 1.2 copy-done
  2.8 0.0 copy-start.1
  2.8 0.7 copy-done.1
  3.5 127.5 %routed_experts.1 = bf16[2,64,3584]{2,1,0:T(8,128)(2,1)S(1)} custom-call(s32[2,64]{1,0:T(2,128)S(1)} %bitcast.8, bf16[32,2,2,128]{3,2,1,0:T(2,128)(2,1)S(1)} %fusion.2.spread_hbm, bf16[2,64,3584]{2,1,0:T(8,128)(2,1)S(1)} %copy-done, bf16[1,3584,512]{2,1,0:T(8,128)(2,1)} %gate_hbm.1, bf16[1,3584,512]{2,1,0:T(8,128)(2,1)} %up_hbm.1, bf16[1,512,3584]{2,1,0:T(8,128)(2,1)} %down_hbm.1), custom_call_target="tpu_custom_call" | custom-call | tf_op jit(solution)/shard_map/routed_experts/pallas_call | solution.py:351
  131.0 0.9 copy.12
  (1 shorter events, 0.0 us)
Async XLA Ops:
  1.6 1.2 copy-start
  2.8 0.7 copy-start.1

commit v5 on v4

--- a/solution.py
+++ b/solution.py
@@ -13,6 +13,7 @@
 RING_X, RING_Y, RING_Z = 4, 4, 8
 PLANE = RING_Y * RING_Z
 CHUNKS = 2
+VMEM_BYTES = 64 * 1024 * 1024
 BF16 = jnp.bfloat16
 F32 = jnp.float32
 LANES = 128
@@ -40,8 +41,8 @@
 
 
 def kernel(
-    ids_hbm, spread_hbm, tokens_ref, gate_hbm, up_hbm, down_hbm, out_hbm,
-    ids_ref, spread_ref, hidden, result, gate, up, down, place, unplace, shares, shares_all, shared, selector,
+    ids_hbm, gain_hbm, router_hbm, tokens_ref, gate_hbm, up_hbm, down_hbm, out_hbm,
+    ids_ref, gain_ref, router_ref, spread_ref, hidden, result, gate, up, down, place, unplace, shares, shares_all, shared, selector,
     outgo, arrive, across, acc_gate, acc_up, acc_logit, acc_square, weight, active, partial, partner_part, back, home,
     small_sem, weight_sem, hidden_sem, out_sem, pass_sem, own_sem, home_own,
     out_send, out_recv, x_send, x_recv, part_send, part_recv, home_send, home_recv,
@@ -98,9 +99,10 @@
     ]
 
     ids_copy = pltpu.make_async_copy(ids_hbm, ids_ref, small_sem.at[0])
-    spread_copy = pltpu.make_async_copy(spread_hbm, spread_ref, small_sem.at[1])
-    ids_copy.start()
-    spread_copy.start()
+    gain_copy = pltpu.make_async_copy(gain_hbm, gain_ref, small_sem.at[1])
+    router_copy = pltpu.make_async_copy(router_hbm.at[0], router_ref, small_sem.at[2])
+    for copy in (ids_copy, gain_copy, router_copy):
+        copy.start()
 
     @pl.when(section == 0)
     def _():
@@ -148,9 +150,25 @@
     entry_at = lax.broadcasted_iota(jnp.int32, (LANES, width), 0)
     selector[...] = jnp.where(entry_at == column_entry, 1.0, 0.0).astype(BF16)
 
-    shared[...] = jnp.zeros_like(shared)
+    gain_copy.wait()
+    router_copy.wait()
+    rows, columns = 4 * PLANE, LANES
+    widen = jnp.where(
+        lax.broadcasted_iota(jnp.int32, (columns, share_width), 0) == lax.broadcasted_iota(jnp.int32, (columns, share_width), 1),
+        1.0, 0.0,
+    ).astype(BF16)
+    router_wide = jnp.dot(widen, router_ref[...], preferred_element_type=F32).astype(BF16)
+    gain_rows = jnp.broadcast_to(gain_ref[...], (8, share_width))
+    gain_wide = lax.dot_general(gain_rows, widen, (((1,), (1,)), ((), ())), preferred_element_type=F32)
+    experts = router_ref.shape[1]
+    row_at = lax.broadcasted_iota(jnp.int32, (rows, experts), 0)
+    expert_at = lax.broadcasted_iota(jnp.int32, (rows, experts), 1)
+    expert_rows = jnp.where(row_at == 2 * expert_at + 1, 1.0, 0.0).astype(BF16)
+    router_rows = lax.dot_general(expert_rows, router_wide, (((1,), (1,)), ((), ())), preferred_element_type=F32)
+    kind = lax.rem(lax.broadcasted_iota(jnp.int32, (rows, columns), 0), 2)
+    spread = jnp.where(kind == 0, gain_wide[0:1, :], router_rows)
+    spread_ref[...] = spread.astype(BF16).reshape(PLANE, 2, 2, LANES)
     pl.semaphore_wait(barrier, PLANE + 3)
-    spread_copy.wait()
     shares[pl.ds(zy, 1)] = spread_ref[pl.ds(zy, 1)]
     for half in HALVES:
         each_peer(
@@ -339,11 +357,7 @@
 def on_device(tokens_in, route_ids, norm_gain, router, gate_proj, up_proj, down_proj):
     micro_count, tok_rows, width = tokens_in.shape
     units = gate_proj.shape[2]
-    share_width = norm_gain.shape[1]
     chunk = width // CHUNKS
-    columns = router[0].T.reshape(PLANE, 2, 1, share_width)
-    gains = jnp.broadcast_to(norm_gain, columns.shape)
-    spread = jnp.pad(jnp.concatenate([gains, columns], axis=2), ((0, 0), (0, 0), (0, 0), (0, LANES - share_width)))
     ids = route_ids.reshape(micro_count, tok_rows)
     any_space = pl.BlockSpec(memory_space=pl.ANY)
     dma = pltpu.SemaphoreType.DMA
@@ -352,10 +366,12 @@
         kernel,
         name="routed_experts",
         out_shape=jax.ShapeDtypeStruct((micro_count, tok_rows, width), BF16),
-        in_specs=[any_space] * 6,
+        in_specs=[any_space] * 7,
         out_specs=any_space,
         scratch_shapes=[
             pltpu.VMEM((MB, tok_rows), jnp.int32),
+            pltpu.VMEM(norm_gain.shape, BF16),
+            pltpu.VMEM(router.shape[1:], BF16),
             pltpu.VMEM((PLANE, 2, 2, LANES), BF16),
             pltpu.VMEM((MB, tok_rows, width), BF16),
             pltpu.VMEM((MB, tok_rows, width), BF16),
@@ -381,14 +397,14 @@
             pltpu.VMEM(grid + (3, HALF, 2, chunk), BF16),
             pltpu.VMEM(grid + (HALF, 2, 2, chunk), BF16),
             pltpu.VMEM((MB, CHUNKS, PLANE, 2, 2, chunk), BF16),
-            dma((2,)), dma((3,)), dma((MB, CHUNKS)), dma((MB, CHUNKS)), dma((MB,)), dma((MB, CHUNKS)), dma((MB, CHUNKS)),
+            dma((3,)), dma((3,)), dma((MB, CHUNKS)), dma((MB, CHUNKS)), dma((MB,)), dma((MB, CHUNKS)), dma((MB, CHUNKS)),
             dma((MB, CHUNKS)), dma(grid), dma(grid + (3,)), dma(grid), dma(grid + (3,)), dma(grid), dma(grid), dma(grid),
             dma((1,)), dma((1,)), dma((3,)), dma((1,)),
         ],
         compiler_params=pltpu.CompilerParams(
-            collective_id=0, has_side_effects=True, vmem_limit_bytes=52 * 1024 * 1024
+            collective_id=0, has_side_effects=True, vmem_limit_bytes=VMEM_BYTES
         ),
-    )(ids, spread, tokens_in, gate_proj, up_proj, down_proj)
+    )(ids, norm_gain, router, tokens_in, gate_proj, up_proj, down_proj)
     return out[None]
 
 

time: 132 us -> 130 us (0.985)
  local copies, waits for them, and re-layouts: 4.28 us -> 2.16 us
    unnamed x5 -> x1, local copies, waits for them, and re-layouts: 2.78 us -> 2.16 us
where the time goes in v5:
time: 130 us
  Pallas kernels  128 us (98%)
  local copies, waits for them, and re-layouts  2.16 us (2%)
    pallas_call x1, Pallas kernels, on_device(): pl.pallas_call(kernel, name='routed_experts', out_shape=jax.ShapeDtypeStr...  128 us

profile of v5, /device:TPU:1, one launch (start us, length us, event | category | flops | bytes accessed | tf_op | source)
XLA Modules:
  0.0 130.0 jit_solution(16582952308367731793)
XLA Ops:
  0.0 127.9 %routed_experts.1 = bf16[2,64,3584]{2,1,0:T(8,128)(2,1)} custom-call(s32[2,64]{1,0:T(2,128)} %bitcast.3, bf16[1,28]{1,0:T(2,128)(2,1)} %gain_hbm.1, bf16[1,28,64]{2,1,0:T(8,128)(2,1)} %router_hbm.1, bf16[2,64,3584]{2,1,0:T(8,128)(2,1)} %tokens_ref.1, bf16[1,3584,512]{2,1,0:T(8,128)(2,1)} %gate_hbm.1, bf16[1,3584,512]{2,1,0:T(8,128)(2,1)} %up_hbm.1, ...), custom_call_target="tpu_custom_call" | custom-call | tf_op jit(solution)/shard_map/routed_experts/pallas_call | solution.py:365
  127.9 2.2 %copy.9 = bf16[1,2,64,3584]{3,2,1,0:T(8,128)(2,1)} copy(bf16[1,2,64,3584]{3,2,1,0:T(8,128)(2,1)} %bitcast.2) | data formatting | bytes 1835008

commit v6 on v5

--- a/solution.py
+++ b/solution.py
@@ -12,7 +12,7 @@
 MB = 2
 RING_X, RING_Y, RING_Z = 4, 4, 8
 PLANE = RING_Y * RING_Z
-CHUNKS = 2
+CHUNKS = 4
 VMEM_BYTES = 64 * 1024 * 1024
 BF16 = jnp.bfloat16
 F32 = jnp.float32
@@ -22,13 +22,19 @@
 HALVES = (0, 1)
 HALF = PLANE // 2
 OWN = HALF - RING_Y
-FIRST = ("N00a", "N01a", "M00a", "M01a")
+FIRST = (
+    "N00a", "N01a", "N02a", "N03a", "M00a", "M01a", "M02a", "M03a",
+)
 ORDER = (
-    "N00b", "M00b", "N01b", "M01b", "N10a", "N11a", "X000", "M10a", "X001a", "M11a", "X010", "X001b",
-    "G000", "G010b", "G001", "A00", "X011", "D000", "D001", "G010a", "G011", "A01", "D010", "D011",
-    "N10b", "M10b", "N11b", "M11b", "X100", "X110b", "X101", "X110a", "X111", "S000", "S001", "S010", "S011",
-    "G100", "G101", "A10", "D100", "D101", "C00", "C01", "G110", "G111", "A11", "D110", "D111",
-    "S100", "S101", "S110", "S111", "C10", "C11",
+    "N00b", "N01b", "M00b", "M01b", "N02b", "N03b", "M02b", "M03b", "N10a", "N11a", "N12a", "N13a", "X000", "X001",
+    "M10a", "M11a", "X002a", "X003a", "M12a", "M13a", "X010", "X011", "X002b", "X003b", "G000", "G001", "G010b",
+    "G011b", "G002", "G003", "A00", "X012", "X013", "D000", "D001", "D002", "D003", "G010a", "G011a", "G012", "G013",
+    "A01", "D010", "D011", "D012", "D013", "N10b", "N11b", "M10b", "M11b", "N12b", "N13b", "M12b", "M13b", "X100",
+    "X101", "X110b", "X111b", "X102", "X103", "X110a", "X111a", "S000", "S001", "S002", "S003", "X112a", "X113a",
+    "S010", "S011", "S012", "S013", "X112b", "X113b", "G100", "G101", "G110b", "G111b", "G102", "G103", "A10", "D100",
+    "D101", "D102", "D103", "C00a", "C01a", "C02a", "C03a", "G110a", "G111a", "G112", "G113", "A11", "D110", "D111",
+    "D112", "D113", "S100", "S101", "S102", "S103", "S110", "S111", "S112", "S113", "C00b", "C01b", "C02b", "C03b",
+    "C10", "C11", "C12", "C13",
 )
 
 
@@ -71,7 +77,8 @@
                 act(k * RING_Y + dy, there, thence)
 
         def body(k, carry):
-            plane(k, 2 * k + 2 - half, 0)
+            far_first = jnp.where(k < 2, 3 + 2 * k, 6 * k - 11) if half else jnp.where(k == 0, 4, 4 * k - 2)
+            plane(k, far_first, 0)
             return carry
 
         lax.fori_loop(0, RING_Z // 2 - 1 + half, body, 0)
@@ -236,7 +243,7 @@
 
     def step_x(m, half, c):
         half_landed(arrive.at[m, half, c], half, out_recv.at[m, half, c], own_sem.at[m, c])
-        for copy in share_rows(m, half, c):
+        for copy in reversed(share_rows(m, half, c)):
             copy.start()
 
     def step_g(m, half, c):
@@ -284,7 +291,7 @@
     def step_d(m, half, c):
         part = jnp.dot(active[half], down[:, pl.ds(c * chunk, chunk)], preferred_element_type=F32) * weight[half, :, 0:1]
         partial[m, half, c] = part.astype(BF16).reshape(4, HALF, 2, chunk)
-        for copy in part_copies(m, half, c):
+        for copy in reversed(part_copies(m, half, c)):
             copy.start()
 
     def step_s(m, half, c):

time: 130 us -> 118 us (0.908)
  Pallas kernels: 128 us -> 116 us
    pallas_call x1, Pallas kernels: 128 us -> 116 us  [on_device(): pl.pallas_call(kernel, name='routed_experts', out_shape=jax.ShapeDtypeStr...]
where the time goes in v6:
time: 118 us
  Pallas kernels  116 us (98%)
  local copies, waits for them, and re-layouts  2.16 us (2%)
    pallas_call x1, Pallas kernels, on_device(): pl.pallas_call(kernel, name='routed_experts', out_shape=jax.ShapeDtypeStr...  116 us

profile of v6, /device:TPU:1, one launch (start us, length us, event | category | flops | bytes accessed | tf_op | source)
XLA Modules:
  0.0 117.7 jit_solution(3767805400132016246)
XLA Ops:
  0.0 115.6 %routed_experts.1 = bf16[2,64,3584]{2,1,0:T(8,128)(2,1)} custom-call(s32[2,64]{1,0:T(2,128)} %bitcast.3, bf16[1,28]{1,0:T(2,128)(2,1)} %gain_hbm.1, bf16[1,28,64]{2,1,0:T(8,128)(2,1)} %router_hbm.1, bf16[2,64,3584]{2,1,0:T(8,128)(2,1)} %tokens_ref.1, bf16[1,3584,512]{2,1,0:T(8,128)(2,1)} %gate_hbm.1, bf16[1,3584,512]{2,1,0:T(8,128)(2,1)} %up_hbm.1, ...), custom_call_target="tpu_custom_call" | custom-call | tf_op jit(solution)/shard_map/routed_experts/pallas_call | solution.py:372
  115.6 2.2 %copy.9 = bf16[1,2,64,3584]{3,2,1,0:T(8,128)(2,1)} copy(bf16[1,2,64,3584]{3,2,1,0:T(8,128)(2,1)} %bitcast.2) | data formatting | bytes 1835008

commit v7 on v6

--- a/solution.py
+++ b/solution.py
@@ -11,6 +11,7 @@
 HE = 1024
 MB = 2
 RING_X, RING_Y, RING_Z = 4, 4, 8
+FAR_Y = (2, 1, 3, 0)
 PLANE = RING_Y * RING_Z
 CHUNKS = 4
 VMEM_BYTES = 64 * 1024 * 1024
@@ -71,7 +72,7 @@
 
     def each_peer(half, act):
         def plane(k, dz, first):
-            for dy in range(first, RING_Y):
+            for dy in [d for d in FAR_Y if d >= first]:
                 there = lax.rem(z + dz, RING_Z) * RING_Y + lax.rem(y + dy, RING_Y)
                 thence = lax.rem(z + RING_Z - dz, RING_Z) * RING_Y + lax.rem(y + RING_Y - dy, RING_Y)
                 act(k * RING_Y + dy, there, thence)

time: 118 us -> 117 us (level)
  no operation moved by 1% of the time
where the time goes in v7:
time: 117 us
  Pallas kernels  115 us (98%)
  local copies, waits for them, and re-layouts  2.16 us (2%)
    pallas_call x1, Pallas kernels, on_device(): pl.pallas_call(kernel, name='routed_experts', out_shape=jax.ShapeDtypeStr...  115 us

profile of v7, /device:TPU:1, one launch (start us, length us, event | category | flops | bytes accessed | tf_op | source)
XLA Modules:
  0.0 117.0 jit_solution(468837051330789395)
XLA Ops:
  0.0 114.8 %routed_experts.1 = bf16[2,64,3584]{2,1,0:T(8,128)(2,1)} custom-call(s32[2,64]{1,0:T(2,128)} %bitcast.3, bf16[1,28]{1,0:T(2,128)(2,1)} %gain_hbm.1, bf16[1,28,64]{2,1,0:T(8,128)(2,1)} %router_hbm.1, bf16[2,64,3584]{2,1,0:T(8,128)(2,1)} %tokens_ref.1, bf16[1,3584,512]{2,1,0:T(8,128)(2,1)} %gate_hbm.1, bf16[1,3584,512]{2,1,0:T(8,128)(2,1)} %up_hbm.1, ...), custom_call_target="tpu_custom_call" | custom-call | tf_op jit(solution)/shard_map/routed_experts/pallas_call | solution.py:373
  114.8 2.2 %copy.9 = bf16[1,2,64,3584]{3,2,1,0:T(8,128)(2,1)} copy(bf16[1,2,64,3584]{3,2,1,0:T(8,128)(2,1)} %bitcast.2) | data formatting | bytes 1835008
